TPU v7x, 32 devices: a whole 2x2x4 slice. The times are simulated.
32 devices in a mesh: dp: 4 (over y, core), seq: 8 (over z, x).
Axes of the slice: x: 2, y: 2, z: 4, core: 2. Of those that a mesh axis runs over, the one named last changes fastest.
Arguments:
- source: bfloat16 [32, 1024, 768], P('dp', 'seq'), may hold values from -6 to 6
- target: bfloat16 [32, 512, 768], P('dp', 'seq'), may hold values from -6 to 6
- source_segments: int32 [32, 1024], P('dp'), may hold values from 0 to 3, as said below
- target_segments: int32 [32, 512], P('dp'), may hold values from 0 to 3, as said below
- cotangent: bfloat16 [32, 512, 768], P('dp', 'seq'), may hold values from -6 to 6
- enc_qkv: bfloat16 [768, 2304], replicated, may hold values from -0.21875 to 0.21875
- enc_out: bfloat16 [768, 768], replicated, may hold values from -6 to 6
- enc_up: bfloat16 [768, 3072], replicated, may hold values from -0.21875 to 0.21875
- enc_down: bfloat16 [3072, 768], replicated, may hold values from -0.109375 to 0.109375
- dec_qkv: bfloat16 [768, 2304], replicated, may hold values from -0.21875 to 0.21875
- dec_out: bfloat16 [768, 768], replicated, may hold values from -2.5 to 2.5
- cross_q: bfloat16 [768, 768], replicated, may hold values from -0.21875 to 0.21875
- cross_kv: bfloat16 [768, 1536], replicated, may hold values from -0.21875 to 0.21875
- cross_out: bfloat16 [768, 768], replicated, may hold values from -6 to 6
- dec_up: bfloat16 [768, 3072], replicated, may hold values from -0.21875 to 0.21875
- dec_down: bfloat16 [3072, 768], replicated, may hold values from -0.109375 to 0.109375
- enc_prefix: bfloat16 [30, 768], replicated, may hold values from -6 to 6
- enc_prefix_in: bfloat16 [768, 512], replicated, may hold values from -0.21875 to 0.21875
- enc_prefix_out: bfloat16 [512, 1536], replicated, may hold values from -0.375 to 0.375
- enc_adapter_down: bfloat16 [768, 512], replicated, may hold values from -0.21875 to 0.21875
- enc_adapter_up: bfloat16 [512, 768], replicated, may hold values from -0.125 to 0.125
- dec_prefix: bfloat16 [30, 768], replicated, may hold values from -6 to 6
- dec_prefix_in: bfloat16 [768, 512], replicated, may hold values from -0.21875 to 0.21875
- dec_prefix_out: bfloat16 [512, 1536], replicated, may hold values from -0.375 to 0.375
- dec_adapter_down: bfloat16 [768, 512], replicated, may hold values from -0.21875 to 0.21875
- dec_adapter_up: bfloat16 [512, 768], replicated, may hold values from -0.125 to 0.125
Outputs:
- out_hidden: bfloat16 [32, 512, 768], P('dp', 'seq')
- source_grad: float32 [32, 1024, 768], P('dp', 'seq')
- target_grad: float32 [32, 512, 768], P('dp', 'seq')
- enc_prefix_grad: float32 [30, 768], P(None, 'seq')
- enc_prefix_in_grad: float32 [768, 512], P('seq')
- enc_prefix_out_grad: float32 [512, 1536], P('seq')
- enc_adapter_down_grad: float32 [768, 512], P('seq')
- enc_adapter_up_grad: float32 [512, 768], P('seq')
- dec_prefix_grad: float32 [30, 768], P(None, 'seq')
- dec_prefix_in_grad: float32 [768, 512], P('seq')
- dec_prefix_out_grad: float32 [512, 1536], P('seq')
- dec_adapter_down_grad: float32 [768, 512], P('seq')
- dec_adapter_up_grad: float32 [512, 768], P('seq')
Inputs may be any that keep to these rules, and one draw needn't show every extreme that they name: `source_segments`: in every row the positions carry the document numbers 0, 1, 2, 3 in this order, never falling, each document at least one position long; document k of a target row belongs to document k of the source row with the same index. `target_segments`: as for source_segments; the longest document of a target row has the number of the longest document of its source row.
All inputs are finite; a program needn't handle non-finite values.
Results may differ from a plain program's by a relative error of at most 0.03.
Values may be sent and summed in bfloat16 or wider, within the bound.
A program may use at most 320 MiB of HBM per device.

v0:
```python
import math

import jax
import jax.numpy as jnp
from jax import lax
from jax.sharding import PartitionSpec as P

HEAD = 64


def project(left, right):
    return jnp.dot(left, right, preferred_element_type=jnp.float32)


def back_through(gradient, weight):
    return jnp.einsum("rln,dn->rld", gradient, weight, preferred_element_type=jnp.float32)


def weight_grad(inputs, gradient):
    return jnp.einsum("rla,rlb->ab", inputs, gradient, preferred_element_type=jnp.float32)


def heads_of(value):
    return value.reshape(value.shape[0], value.shape[1], -1, HEAD)


def rows_of(value):
    return value.reshape(value.shape[0], value.shape[1], -1)


def normalize(value):
    centered = value - jnp.mean(value, axis=-1, keepdims=True)
    inverse = lax.rsqrt(jnp.mean(centered * centered, axis=-1, keepdims=True) + 1e-05)
    return (centered * inverse, inverse)


def normalize_back(gradient, normed, inverse):
    return (
        gradient
        - jnp.mean(gradient, axis=-1, keepdims=True)
        - normed * jnp.mean(gradient * normed, axis=-1, keepdims=True)
    ) * inverse


def gelu_act(value):
    return jax.nn.gelu(value, approximate=True)


def gelu_back(value, gradient):
    return jax.vjp(gelu_act, value)[1](gradient)[0]


def score_parts(query_heads, key_heads, allowed, prefix_keys):
    score_scale = 1.0 / math.sqrt(HEAD)
    scores = (
        jnp.einsum("rqhe,rkhe->rhqk", query_heads, key_heads, preferred_element_type=jnp.float32)
        * score_scale
    )
    scores = jnp.where(allowed[:, None], scores, -1e30)
    if prefix_keys is None:
        return (scores, None)
    extra = (
        jnp.einsum("rqhe,phe->rhqp", query_heads, prefix_keys, preferred_element_type=jnp.float32)
        * score_scale
    )
    return (scores, extra)


def attend_forward(query_heads, key_heads, value_heads, allowed, prefix_keys, prefix_values):
    scores, extra = score_parts(query_heads, key_heads, allowed, prefix_keys)
    row_peak = jnp.max(scores, axis=-1)
    if extra is not None:
        row_peak = jnp.maximum(row_peak, jnp.max(extra, axis=-1))
    weights = jnp.exp(scores - row_peak[..., None])
    row_total = jnp.sum(weights, axis=-1)
    if extra is not None:
        extra_weights = jnp.exp(extra - row_peak[..., None])
        row_total = row_total + jnp.sum(extra_weights, axis=-1)
    context = jnp.einsum(
        "rhqk,rkhe->rqhe",
        (weights / row_total[..., None]).astype(jnp.bfloat16),
        value_heads,
        preferred_element_type=jnp.float32,
    )
    if extra is not None:
        context = context + jnp.einsum(
            "rhqp,phe->rqhe",
            (extra_weights / row_total[..., None]).astype(jnp.bfloat16),
            prefix_values,
            preferred_element_type=jnp.float32,
        )
    return (context, row_peak + jnp.log(row_total))


def attend_backward(
    query_heads, key_heads, value_heads, allowed, prefix_keys, prefix_values, row_lse, context_grad
):
    score_scale = 1.0 / math.sqrt(HEAD)
    scores, extra = score_parts(query_heads, key_heads, allowed, prefix_keys)
    probabilities = jnp.exp(scores - row_lse[..., None])
    prob_grad = jnp.einsum(
        "rqhe,rkhe->rhqk", context_grad, value_heads, preferred_element_type=jnp.float32
    )
    row_delta = jnp.sum(probabilities * prob_grad, axis=-1)
    if extra is not None:
        extra_probs = jnp.exp(extra - row_lse[..., None])
        extra_grad = jnp.einsum(
            "rqhe,phe->rhqp", context_grad, prefix_values, preferred_element_type=jnp.float32
        )
        row_delta = row_delta + jnp.sum(extra_probs * extra_grad, axis=-1)
    score_grad = (probabilities * (prob_grad - row_delta[..., None])).astype(jnp.bfloat16)
    query_grad = jnp.einsum(
        "rhqk,rkhe->rqhe", score_grad, key_heads, preferred_element_type=jnp.float32
    )
    key_grad = (
        jnp.einsum("rhqk,rqhe->rkhe", score_grad, query_heads, preferred_element_type=jnp.float32)
        * score_scale
    )
    value_grad = jnp.einsum(
        "rhqk,rqhe->rkhe",
        probabilities.astype(jnp.bfloat16),
        context_grad,
        preferred_element_type=jnp.float32,
    )
    prefix_grads = None
    if extra is not None:
        extra_score = (extra_probs * (extra_grad - row_delta[..., None])).astype(jnp.bfloat16)
        query_grad = query_grad + jnp.einsum(
            "rhqp,phe->rqhe", extra_score, prefix_keys, preferred_element_type=jnp.float32
        )
        prefix_grads = (
            jnp.einsum(
                "rhqp,rqhe->phe", extra_score, query_heads, preferred_element_type=jnp.float32
            )
            * score_scale,
            jnp.einsum(
                "rhqp,rqhe->phe",
                extra_probs.astype(jnp.bfloat16),
                context_grad,
                preferred_element_type=jnp.float32,
            ),
        )
    return (query_grad * score_scale, key_grad, value_grad, prefix_grads)


def select_head(value, head_index, axis):
    if value is None:
        return None
    return lax.dynamic_slice_in_dim(value, head_index, 1, axis)


def attend_forward_blocks(query_heads, key_heads, value_heads, allowed, prefix_keys, prefix_values):

    def one_head(head_index):
        return attend_forward(
            select_head(query_heads, head_index, 2),
            select_head(key_heads, head_index, 2),
            select_head(value_heads, head_index, 2),
            allowed,
            select_head(prefix_keys, head_index, 1),
            select_head(prefix_values, head_index, 1),
        )

    context, row_lse = lax.map(one_head, jnp.arange(query_heads.shape[2]))
    return (jnp.moveaxis(context[:, :, :, 0], 0, 2), jnp.moveaxis(row_lse[:, :, 0], 0, 1))


def attend_backward_blocks(
    query_heads, key_heads, value_heads, allowed, prefix_keys, prefix_values, row_lse, context_grad
):

    def one_head(head_index):
        return attend_backward(
            select_head(query_heads, head_index, 2),
            select_head(key_heads, head_index, 2),
            select_head(value_heads, head_index, 2),
            allowed,
            select_head(prefix_keys, head_index, 1),
            select_head(prefix_values, head_index, 1),
            select_head(row_lse, head_index, 1),
            select_head(context_grad, head_index, 2),
        )

    query_grad, key_grad, value_grad, prefix_grads = lax.map(
        one_head, jnp.arange(query_heads.shape[2])
    )
    query_grad = jnp.moveaxis(query_grad[:, :, :, 0], 0, 2)
    key_grad = jnp.moveaxis(key_grad[:, :, :, 0], 0, 2)
    value_grad = jnp.moveaxis(value_grad[:, :, :, 0], 0, 2)
    if prefix_grads is not None:
        prefix_grads = (
            jnp.moveaxis(prefix_grads[0][:, :, 0], 0, 1),
            jnp.moveaxis(prefix_grads[1][:, :, 0], 0, 1),
        )
    return (query_grad, key_grad, value_grad, prefix_grads)


def cross_gathered(cross_query, memory_pairs, allowed, collect):
    model_width = cross_query.shape[2]
    memory_all = collect(memory_pairs)
    context, row_lse = attend_forward_blocks(
        heads_of(cross_query),
        heads_of(memory_all[..., :model_width]),
        heads_of(memory_all[..., model_width:]),
        allowed,
        None,
        None,
    )
    return (rows_of(context), (cross_query, memory_all, row_lse))


def cross_gathered_back(context_grad, kept, allowed, spread):
    cross_query, memory_all, row_lse = kept
    model_width = cross_query.shape[2]
    query_grad, key_grad, value_grad, unused_prefix = attend_backward_blocks(
        heads_of(cross_query),
        heads_of(memory_all[..., :model_width]),
        heads_of(memory_all[..., model_width:]),
        allowed,
        None,
        None,
        row_lse,
        heads_of(context_grad),
    )
    pair_grad = spread(jnp.concatenate([rows_of(key_grad), rows_of(value_grad)], axis=-1))
    return (rows_of(query_grad), pair_grad)


def prefix_forward(prefix, prefix_in, prefix_out):
    hidden = jnp.tanh(jnp.dot(prefix, prefix_in, preferred_element_type=jnp.float32))
    pair_rows = jnp.dot(hidden, prefix_out.astype(jnp.float32), precision=lax.Precision.HIGHEST)
    return (hidden, pair_rows.astype(jnp.bfloat16))


def prefix_backward(prefix, prefix_in, prefix_out, hidden, pair_grad):
    out_grad = jnp.dot(hidden.T, pair_grad, precision=lax.Precision.HIGHEST)
    hidden_grad = jnp.dot(
        pair_grad, prefix_out.astype(jnp.float32).T, precision=lax.Precision.HIGHEST
    ) * (1.0 - hidden * hidden)
    in_grad = jnp.dot(prefix.astype(jnp.float32).T, hidden_grad, precision=lax.Precision.HIGHEST)
    embed_grad = jnp.dot(
        hidden_grad, prefix_in.astype(jnp.float32).T, precision=lax.Precision.HIGHEST
    )
    return (embed_grad, in_grad, out_grad)


def prefix_heads(prefix_pairs):
    model_width = prefix_pairs.shape[1] // 2
    prefix_count = prefix_pairs.shape[0]
    return (
        prefix_pairs[:, :model_width].reshape(prefix_count, -1, HEAD),
        prefix_pairs[:, model_width:].reshape(prefix_count, -1, HEAD),
    )


def self_forward(hidden, hidden_low, qkv_weight, out_weight, prefix_pairs, allowed, collect):
    model_width = hidden.shape[2]
    qkv_rows = project(hidden_low, qkv_weight).astype(jnp.bfloat16)
    query_rows = qkv_rows[..., :model_width]
    pair_rows = collect(qkv_rows[..., model_width:])
    prefix_keys, prefix_values = prefix_heads(prefix_pairs)
    context, row_lse = attend_forward_blocks(
        heads_of(query_rows),
        heads_of(pair_rows[..., :model_width]),
        heads_of(pair_rows[..., model_width:]),
        allowed,
        prefix_keys,
        prefix_values,
    )
    context_low = rows_of(context).astype(jnp.bfloat16)
    normed, inverse = normalize(hidden + project(context_low, out_weight))
    return (normed, (query_rows, pair_rows, row_lse, normed, inverse))


def self_backward(gradient, stored, qkv_weight, out_weight, prefix_pairs, allowed, spread):
    query_rows, pair_rows, row_lse, normed, inverse = stored
    model_width = query_rows.shape[2]
    prefix_count = prefix_pairs.shape[0]
    prefix_keys, prefix_values = prefix_heads(prefix_pairs)
    summed_grad = normalize_back(gradient, normed, inverse)
    context_grad = back_through(summed_grad.astype(jnp.bfloat16), out_weight).astype(jnp.bfloat16)
    query_grad, key_grad, value_grad, prefix_grads = attend_backward_blocks(
        heads_of(query_rows),
        heads_of(pair_rows[..., :model_width]),
        heads_of(pair_rows[..., model_width:]),
        allowed,
        prefix_keys,
        prefix_values,
        row_lse,
        heads_of(context_grad),
    )
    pair_grad = spread(jnp.concatenate([rows_of(key_grad), rows_of(value_grad)], axis=-1))
    qkv_grad = jnp.concatenate([rows_of(query_grad), pair_grad], axis=-1).astype(jnp.bfloat16)
    hidden_grad = summed_grad + back_through(qkv_grad, qkv_weight)
    prefix_pair_grad = jnp.concatenate(
        [
            prefix_grads[0].reshape(prefix_count, model_width),
            prefix_grads[1].reshape(prefix_count, model_width),
        ],
        axis=-1,
    )
    return (hidden_grad, prefix_pair_grad)


def feed_forward(hidden, up_weight, down_weight, adapter_down, adapter_up):
    hidden_low = hidden.astype(jnp.bfloat16)
    inner_pre = project(hidden_low, up_weight)
    active = gelu_act(inner_pre).astype(jnp.bfloat16)
    narrow = project(hidden_low, adapter_down)
    narrow_act = gelu_act(narrow).astype(jnp.bfloat16)
    summed = hidden + project(active, down_weight) + 4.0 * project(narrow_act, adapter_up)
    normed, inverse = normalize(summed)
    return (normed, (hidden_low, inner_pre, narrow, narrow_act, normed, inverse))


def feed_backward(gradient, stored, up_weight, down_weight, adapter_down, adapter_up):
    hidden_low, inner_pre, narrow, narrow_act, normed, inverse = stored
    summed_grad = normalize_back(gradient, normed, inverse)
    main_grad = summed_grad.astype(jnp.bfloat16)
    side_grad = (4.0 * summed_grad).astype(jnp.bfloat16)
    adapter_up_grad = weight_grad(narrow_act, side_grad)
    narrow_grad = gelu_back(narrow, back_through(side_grad, adapter_up)).astype(jnp.bfloat16)
    adapter_down_grad = weight_grad(hidden_low, narrow_grad)
    inner_grad = gelu_back(inner_pre, back_through(main_grad, down_weight)).astype(jnp.bfloat16)
    hidden_grad = (
        summed_grad + back_through(inner_grad, up_weight) + back_through(narrow_grad, adapter_down)
    )
    return (hidden_grad, adapter_down_grad, adapter_up_grad)


def shards(
    source,
    target,
    source_segments,
    target_segments,
    cotangent,
    enc_qkv,
    enc_out,
    enc_up,
    enc_down,
    dec_qkv,
    dec_out,
    cross_q,
    cross_kv,
    cross_out,
    dec_up,
    dec_down,
    enc_prefix,
    enc_prefix_in,
    enc_prefix_out,
    enc_adapter_down,
    enc_adapter_up,
    dec_prefix,
    dec_prefix_in,
    dec_prefix_out,
    dec_adapter_down,
    dec_adapter_up,
):
    seq_place = lax.axis_index("seq")
    source_local = source.shape[1]
    target_local = target.shape[1]
    source_own = lax.dynamic_slice_in_dim(
        source_segments, seq_place * source_local, source_local, 1
    )
    target_own = lax.dynamic_slice_in_dim(
        target_segments, seq_place * target_local, target_local, 1
    )
    query_start = seq_place * target_local

    def enc_collect(pieces):
        return lax.all_gather(pieces, "seq", axis=1, tiled=True)

    def enc_spread(pieces):
        return lax.psum_scatter(
            pieces.astype(jnp.bfloat16), "seq", scatter_dimension=1, tiled=True
        ).astype(jnp.float32)

    def dec_collect(pieces):
        return lax.all_gather(pieces, "seq", axis=1, tiled=True)

    def dec_spread(pieces):
        return lax.psum_scatter(
            pieces.astype(jnp.bfloat16), "seq", scatter_dimension=1, tiled=True
        ).astype(jnp.float32)

    cross_allowed = target_own[:, :, None] == source_segments[:, None, :]

    def memory_collect(pieces):
        return lax.all_gather(pieces, "seq", axis=1, tiled=True)

    def memory_spread(pieces):
        return lax.psum_scatter(
            pieces.astype(jnp.bfloat16), "seq", scatter_dimension=1, tiled=True
        ).astype(jnp.float32)

    enc_allowed = source_own[:, :, None] == source_segments[:, None, :]
    query_place = query_start + jnp.arange(target_own.shape[1])
    key_place = jnp.arange(target_segments.shape[1])
    dec_allowed = (target_own[:, :, None] == target_segments[:, None, :]) & (
        key_place[None, None, :] <= query_place[None, :, None]
    )
    enc_hidden, enc_pairs = prefix_forward(enc_prefix, enc_prefix_in, enc_prefix_out)
    dec_hidden, dec_pairs = prefix_forward(dec_prefix, dec_prefix_in, dec_prefix_out)
    encoded_mid, encoded_stored = self_forward(
        source.astype(jnp.float32), source, enc_qkv, enc_out, enc_pairs, enc_allowed, enc_collect
    )
    memory, memory_stored = feed_forward(
        encoded_mid, enc_up, enc_down, enc_adapter_down, enc_adapter_up
    )
    decoded_mid, decoded_stored = self_forward(
        target.astype(jnp.float32), target, dec_qkv, dec_out, dec_pairs, dec_allowed, dec_collect
    )
    cross_query = project(decoded_mid.astype(jnp.bfloat16), cross_q).astype(jnp.bfloat16)
    memory_pairs = project(memory.astype(jnp.bfloat16), cross_kv).astype(jnp.bfloat16)
    cross_context, cross_kept = cross_gathered(
        cross_query, memory_pairs, cross_allowed, memory_collect
    )
    crossed, crossed_inverse = normalize(
        decoded_mid + project(cross_context.astype(jnp.bfloat16), cross_out)
    )
    output_wide, output_stored = feed_forward(
        crossed, dec_up, dec_down, dec_adapter_down, dec_adapter_up
    )
    crossed_grad, dec_adapter_down_grad, dec_adapter_up_grad = feed_backward(
        cotangent.astype(jnp.float32),
        output_stored,
        dec_up,
        dec_down,
        dec_adapter_down,
        dec_adapter_up,
    )
    cross_sum_grad = normalize_back(crossed_grad, crossed, crossed_inverse)
    context_grad = back_through(cross_sum_grad.astype(jnp.bfloat16), cross_out).astype(jnp.bfloat16)
    cross_query_grad, memory_pair_grad = cross_gathered_back(
        context_grad, cross_kept, cross_allowed, memory_spread
    )
    memory_grad = back_through(memory_pair_grad.astype(jnp.bfloat16), cross_kv)
    decoded_grad = cross_sum_grad + back_through(cross_query_grad.astype(jnp.bfloat16), cross_q)
    target_grad, dec_pair_grad = self_backward(
        decoded_grad, decoded_stored, dec_qkv, dec_out, dec_pairs, dec_allowed, dec_spread
    )
    encoded_grad, enc_adapter_down_grad, enc_adapter_up_grad = feed_backward(
        memory_grad, memory_stored, enc_up, enc_down, enc_adapter_down, enc_adapter_up
    )
    source_grad, enc_pair_grad = self_backward(
        encoded_grad, encoded_stored, enc_qkv, enc_out, enc_pairs, enc_allowed, enc_spread
    )
    enc_prefix_grad, enc_prefix_in_grad, enc_prefix_out_grad = prefix_backward(
        enc_prefix, enc_prefix_in, enc_prefix_out, enc_hidden, enc_pair_grad
    )
    dec_prefix_grad, dec_prefix_in_grad, dec_prefix_out_grad = prefix_backward(
        dec_prefix, dec_prefix_in, dec_prefix_out, dec_hidden, dec_pair_grad
    )
    shares = (
        lax.psum_scatter(
            enc_prefix_grad.astype(jnp.bfloat16), "seq", scatter_dimension=1, tiled=True
        ).astype(jnp.float32),
        lax.psum_scatter(
            enc_prefix_in_grad.astype(jnp.bfloat16), "seq", scatter_dimension=0, tiled=True
        ).astype(jnp.float32),
        lax.psum_scatter(
            enc_prefix_out_grad.astype(jnp.bfloat16), "seq", scatter_dimension=0, tiled=True
        ).astype(jnp.float32),
        lax.psum_scatter(
            enc_adapter_down_grad.astype(jnp.bfloat16), "seq", scatter_dimension=0, tiled=True
        ).astype(jnp.float32),
        lax.psum_scatter(
            enc_adapter_up_grad.astype(jnp.bfloat16), "seq", scatter_dimension=0, tiled=True
        ).astype(jnp.float32),
        lax.psum_scatter(
            dec_prefix_grad.astype(jnp.bfloat16), "seq", scatter_dimension=1, tiled=True
        ).astype(jnp.float32),
        lax.psum_scatter(
            dec_prefix_in_grad.astype(jnp.bfloat16), "seq", scatter_dimension=0, tiled=True
        ).astype(jnp.float32),
        lax.psum_scatter(
            dec_prefix_out_grad.astype(jnp.bfloat16), "seq", scatter_dimension=0, tiled=True
        ).astype(jnp.float32),
        lax.psum_scatter(
            dec_adapter_down_grad.astype(jnp.bfloat16), "seq", scatter_dimension=0, tiled=True
        ).astype(jnp.float32),
        lax.psum_scatter(
            dec_adapter_up_grad.astype(jnp.bfloat16), "seq", scatter_dimension=0, tiled=True
        ).astype(jnp.float32),
    )
    totals = (
        lax.psum(shares[0].astype(jnp.bfloat16), "dp").astype(jnp.float32),
        lax.psum(shares[1].astype(jnp.bfloat16), "dp").astype(jnp.float32),
        lax.psum(shares[2].astype(jnp.bfloat16), "dp").astype(jnp.float32),
        lax.psum(shares[3].astype(jnp.bfloat16), "dp").astype(jnp.float32),
        lax.psum(shares[4].astype(jnp.bfloat16), "dp").astype(jnp.float32),
        lax.psum(shares[5].astype(jnp.bfloat16), "dp").astype(jnp.float32),
        lax.psum(shares[6].astype(jnp.bfloat16), "dp").astype(jnp.float32),
        lax.psum(shares[7].astype(jnp.bfloat16), "dp").astype(jnp.float32),
        lax.psum(shares[8].astype(jnp.bfloat16), "dp").astype(jnp.float32),
        lax.psum(shares[9].astype(jnp.bfloat16), "dp").astype(jnp.float32),
    )
    return (
        output_wide.astype(jnp.bfloat16),
        source_grad,
        target_grad,
        totals[0],
        totals[1],
        totals[2],
        totals[3],
        totals[4],
        totals[5],
        totals[6],
        totals[7],
        totals[8],
        totals[9],
    )


def solution(mesh):
    in_specs = (
        P("dp", "seq", None),
        P("dp", "seq", None),
        P("dp", None),
        P("dp", None),
        P("dp", "seq", None),
        P(),
        P(),
        P(),
        P(),
        P(),
        P(),
        P(),
        P(),
        P(),
        P(),
        P(),
        P(),
        P(),
        P(),
        P(),
        P(),
        P(),
        P(),
        P(),
        P(),
        P(),
    )
    out_specs = (
        P("dp", "seq", None),
        P("dp", "seq", None),
        P("dp", "seq", None),
        P(None, "seq"),
        P("seq", None),
        P("seq", None),
        P("seq", None),
        P("seq", None),
        P(None, "seq"),
        P("seq", None),
        P("seq", None),
        P("seq", None),
        P("seq", None),
    )
    return jax.shard_map(shards, mesh=mesh, in_specs=in_specs, out_specs=out_specs, check_vma=False)
```

profile of v0, /device:TPU:0, one launch (start us, length us, event | category | flops | bytes accessed | tf_op | source)
XLA Modules:
  0.0 3743.8 jit_solution(9265262268865600640)
XLA Ops:
  46.6 455.8 %all-gather.6.cloned.1.call-done = bf16[8,1024,1536]{2,1,0:T(8,128)(2,1)} async-done(((bf16[8,128,1536]{2,1,0:T(8,128)(2,1)}), bf16[8,1024,1536]{2,1,0:T(8,128)(2,1)}) %all-gather.6.cloned.1.call-update) | async-done | bytes 25165840 | tf_op jit(solution)/shard_map/all_gather | solution.py:371
  576.7 145.4 %while.93 = (s32[]{:T(128)}, bf16[12,8,128,1,64]{2,4,0,1,3:T(8,128)(2,1)}, f32[12,8,1,128]{3,1,2,0:T(8,128)}, s32[12]{0:T(128)S(1)}, bf16[8,1024,12,64]{1,3,0,2:...) while((s32[]{:T(128)}, ...), condition=%wide.region_13.14_spmd.clone, body=%wide.region_8.0_spmd.clone.sunk | while | flops 292307968 | bytes 16432343 | solution.py:164
  818.9 111.8 %while.92 = (s32[]{:T(128)}, bf16[12,8,64,1,64]{2,4,1,3,0:T(8,128)(2,1)}, f32[12,8,1,64]{3,1,2,0:T(8,128)}, s32[12]{0:T(128)S(1)}, bf16[8,512,12,64]{1,3,0,2:T(8...) while((s32[]{:T(128)}, ...), condition=%wide.region_5.6_spmd.clone, body=%wide.region_0.5_spmd.clone.sunk | while | flops 73802240 | bytes 5274819 | solution.py:164
  951.5 284.1 %all-gather.8.cloned.1.call-done = bf16[8,1024,1536]{2,1,0:T(8,128)(2,1)} async-done(((bf16[8,128,1536]{2,1,0:T(8,128)(2,1)}), bf16[8,1024,1536]{2,1,0:T(8,128)(2,1)}) %all-gather.8.cloned.1.call-update) | async-done | bytes 25165840 | tf_op jit(solution)/shard_map/all_gather | solution.py:389
  1309.6 95.7 %while.94 = (s32[]{:T(128)}, bf16[12,8,64,1,64]{2,4,1,3,0:T(8,128)(2,1)}, f32[12,8,1,64]{3,1,2,0:T(8,128)}, s32[12]{0:T(128)S(1)}, bf16[8,1024,12,64]{1,3,0,2:T(...) while((s32[]{:T(128)}, ...), condition=%wide.region_21.22_spmd.clone, body=%wide.region_18.21_spmd.clone.sunk | while | flops 138935808 | bytes 8837287 | solution.py:164
  1474.9 174.7 %while.95 = (s32[]{:T(128)}, bf16[12,8,64,1,64]{2,4,1,3,0:T(8,128)(2,1)}, bf16[12,8,1024,1,64]{2,4,0,1,3:T(8,128)(2,1)}, bf16[12,8,1024,1,64]{2,4,0,1,3:T(8,128)...) while((s32[]{:T(128)}, ...), condition=%wide.region_32.33_spmd.clone, body=%wide.region_30.32_spmd.clone.sunk | while | flops 341343744 | bytes 24035048 | solution.py:184
  1649.6 24.9 pad_maximum_fusion
  1674.4 32.7 copy.226
  1707.1 24.9 copy.273
  1757.6 232.5 %while.97 = (s32[]{:T(128)}, bf16[12,8,64,1,64]{2,4,1,3,0:T(8,128)(2,1)}, bf16[12,8,512,1,64]{2,4,0,1,3:T(8,128)(2,1)}, bf16[12,8,512,1,64]{2,4,0,1,3:T(8,128)(2...) while((s32[]{:T(128)}, ...), condition=%wide.region_48.49_spmd.clone, body=%wide.region_45.48_spmd.clone.sunk | while | flops 180938112 | bytes 13705983 | solution.py:184
  2007.1 128.8 %reduce-scatter.40.cloned.1.call-done = bf16[128,12288]{1,0:T(8,128)(2,1)} async-done(((bf16[1024,12288]{1,0:T(8,128)(2,1)}), bf16[128,12288]{1,0:T(8,128)(2,1)}) %reduce-scatter.40.cloned.1.call-update) | async-done | bytes 3145744
  2146.0 20.6 fusion.235
  2196.4 272.8 %while.96 = (s32[]{:T(128)}, bf16[12,8,128,1,64]{2,4,0,1,3:T(8,128)(2,1)}, bf16[12,8,1024,1,64]{2,4,0,1,3:T(8,128)(2,1)}, bf16[12,8,1024,1,64]{2,4,0,1,3:T(8,128...) while((s32[]{:T(128)}, ...), condition=%wide.region_41.42_spmd.clone, body=%wide.region_38.41_spmd.clone.sunk | while | flops 702137216 | bytes 41831188 | solution.py:184
  2584.9 27.7 reduce-scatter.38.cloned.1.call-done
  2612.6 65.1 %reduce-scatter.36.cloned.1.call-done = bf16[96,512]{1,0:T(8,128)(2,1)} async-done(((bf16[768,512]{1,0:T(8,128)(2,1)}), bf16[96,512]{1,0:T(8,128)(2,1)}) %reduce-scatter.36.cloned.1.call-update) | async-done | bytes 98320 | tf_op jit(solution)/shard_map/reduce_scatter | solution.py:479
  2677.7 67.3 %reduce-scatter.34.cloned.1.call-done = bf16[64,1536]{1,0:T(8,128)(2,1)} async-done(((bf16[512,1536]{1,0:T(8,128)(2,1)}), bf16[64,1536]{1,0:T(8,128)(2,1)}) %reduce-scatter.34.cloned.1.call-update) | async-done | bytes 196624 | tf_op jit(solution)/shard_map/reduce_scatter | solution.py:476
  2745.0 64.9 %reduce-scatter.32.cloned.1.call-done = bf16[64,768]{1,0:T(8,128)(2,1)} async-done(((bf16[512,768]{1,0:T(8,128)(2,1)}), bf16[64,768]{1,0:T(8,128)(2,1)}) %reduce-scatter.32.cloned.1.call-update) | async-done | bytes 98320 | tf_op jit(solution)/shard_map/reduce_scatter | solution.py:467
  2809.9 65.2 %reduce-scatter.30.cloned.1.call-done = bf16[96,512]{1,0:T(8,128)(2,1)} async-done(((bf16[768,512]{1,0:T(8,128)(2,1)}), bf16[96,512]{1,0:T(8,128)(2,1)}) %reduce-scatter.30.cloned.1.call-update) | async-done | bytes 98320 | tf_op jit(solution)/shard_map/reduce_scatter | solution.py:464
  2875.1 68.1 %reduce-scatter.28.cloned.1.call-done = bf16[64,1536]{1,0:T(8,128)(2,1)} async-done(((bf16[512,1536]{1,0:T(8,128)(2,1)}), bf16[64,1536]{1,0:T(8,128)(2,1)}) %reduce-scatter.28.cloned.1.call-update) | async-done | bytes 196624 | tf_op jit(solution)/shard_map/reduce_scatter | solution.py:461
  2972.2 35.0 reduce-scatter.46.cloned.1.call-done
  3008.6 208.4 %reduce-scatter.26.cloned.1.call-done = bf16[8,64,1536]{2,1,0:T(8,128)(2,1)} async-done(((bf16[8,512,1536]{2,1,0:T(8,128)(2,1)}), bf16[8,64,1536]{2,1,0:T(8,128)(2,1)}) %reduce-scatter.26.cloned.1.call-update) | async-done | bytes 1572880 | tf_op jit(solution)/shard_map/reduce_scatter | solution.py:382
  3226.4 54.5 %reduce-scatter.42.cloned.1.call-done = bf16[96,30]{1,0:T(8,128)(2,1)} async-done(((bf16[768,30]{1,0:T(8,128)(2,1)}), bf16[96,30]{1,0:T(8,128)(2,1)}) %reduce-scatter.42.cloned.1.call-update) | async-done | bytes 5776
  3296.7 24.4 all-reduce.4.cloned.1.call-done
  3333.4 395.9 %reduce-scatter.24.cloned.1.call-done = bf16[8,128,1536]{2,1,0:T(8,128)(2,1)} async-done(((bf16[8,1024,1536]{2,1,0:T(8,128)(2,1)}), bf16[8,128,1536]{2,1,0:T(8,128)(2,1)}) %reduce-scatter.24.cloned.1.call-update) | async-done | bytes 3145744 | tf_op jit(solution)/shard_map/reduce_scatter | solution.py:374
  (1200 shorter events, 1537.1 us)
Async XLA Ops:
  7.2 495.2 %all-gather.6.cloned.1.call-start = ((), (), s32[]{:S(2)}) async-start(), calls=%async_computation.14 | async-start | bytes 28311552 | tf_op jit(solution)/shard_map/all_gather | solution.py:371
  19.1 757.3 %all-gather.4.cloned.1.call-start = ((), (), s32[]{:S(2)}) async-start(), calls=%async_computation.13 | async-start | bytes 14155776 | tf_op jit(solution)/shard_map/all_gather | solution.py:379
  26.2 1209.4 %all-gather.8.cloned.1.call-start = ((), (), s32[]{:S(2)}) async-start(), calls=%async_computation.15 | async-start | bytes 28311552 | tf_op jit(solution)/shard_map/all_gather | solution.py:389
  754.5 1381.4 %reduce-scatter.40.cloned.1.call-start = ((), (), s32[]{:S(2)}) async-start(), calls=%async_computation.24 | async-start | bytes 28311552
  941.6 471.9 %copy-start.56 = (f32[8,64]{1,0:T(8,128)}, f32[8,64]{1,0:T(8,128)S(1)}, u32[]{:S(2)}) copy-start(f32[8,64]{1,0:T(8,128)S(1)} %broadcast_multiply_fusion.14) | copy-start | bytes 6148
  942.7 470.7 %copy-start.64 = (f32[8,64]{1,0:T(8,128)}, f32[8,64]{1,0:T(8,128)S(1)}, u32[]{:S(2)}) copy-start(f32[8,64]{1,0:T(8,128)S(1)} %add_rsqrt_fusion.4) | copy-start | bytes 6148
  1427.6 21.9 copy-start.54
  1732.0 816.2 %reduce-scatter.48.cloned.1.call-start = ((), (), s32[]{:S(2)}) async-start(), calls=%async_computation.28 | async-start | bytes 884736
  2007.1 576.2 %reduce-scatter.44.cloned.1.call-start = ((), (), s32[]{:S(2)}) async-start(), calls=%async_computation.26 | async-start | bytes 884736
  2486.1 126.5 %reduce-scatter.38.cloned.1.call-start = ((), (), s32[]{:S(2)}) async-start(), calls=%async_computation.23 | async-start | bytes 884736 | tf_op jit(solution)/shard_map/reduce_scatter | solution.py:482
  2490.2 187.5 %reduce-scatter.36.cloned.1.call-start = ((), (), s32[]{:S(2)}) async-start(), calls=%async_computation.22 | async-start | bytes 884736 | tf_op jit(solution)/shard_map/reduce_scatter | solution.py:479
  2493.0 251.9 %reduce-scatter.34.cloned.1.call-start = ((), (), s32[]{:S(2)}) async-start(), calls=%async_computation.21 | async-start | bytes 1769472 | tf_op jit(solution)/shard_map/reduce_scatter | solution.py:476
  2498.3 311.6 %reduce-scatter.32.cloned.1.call-start = ((), (), s32[]{:S(2)}) async-start(), calls=%async_computation.20 | async-start | bytes 884736 | tf_op jit(solution)/shard_map/reduce_scatter | solution.py:467
  2503.1 372.1 %reduce-scatter.30.cloned.1.call-start = ((), (), s32[]{:S(2)}) async-start(), calls=%async_computation.19 | async-start | bytes 884736 | tf_op jit(solution)/shard_map/reduce_scatter | solution.py:464
  2506.8 436.5 %reduce-scatter.28.cloned.1.call-start = ((), (), s32[]{:S(2)}) async-start(), calls=%async_computation.18 | async-start | bytes 1769472 | tf_op jit(solution)/shard_map/reduce_scatter | solution.py:461
  2511.6 495.5 %reduce-scatter.46.cloned.1.call-start = ((), (), s32[]{:S(2)}) async-start(), calls=%async_computation.27 | async-start | bytes 221184
  2533.2 683.8 %reduce-scatter.26.cloned.1.call-start = ((), (), s32[]{:S(2)}) async-start(), calls=%async_computation.17 | async-start | bytes 14155776 | tf_op jit(solution)/shard_map/reduce_scatter | solution.py:382
  2543.9 737.1 %reduce-scatter.42.cloned.1.call-start = ((), (), s32[]{:S(2)}) async-start(), calls=%async_computation.25 | async-start | bytes 221184
  2548.2 772.9 %all-reduce.4.cloned.1.call-start = ((), (), s32[]{:S(2)}) async-start(), calls=%async_computation.29 | async-start | bytes 2097152 | tf_op jit(solution)/shard_map/psum | solution.py:488
  2943.3 785.9 %reduce-scatter.24.cloned.1.call-start = ((), (), s32[]{:S(2)}) async-start(), calls=%async_computation.16 | async-start | bytes 28311552 | tf_op jit(solution)/shard_map/reduce_scatter | solution.py:374
  2968.3 248.7 %copy-start.58 = (f32[8,64]{1,0:T(8,128)S(1)}, f32[8,64]{1,0:T(8,128)}, u32[]{:S(2)}) copy-start(f32[8,64]{1,0:T(8,128)} %copy-done.56) | copy-start | bytes 6148
  2968.3 248.7 %copy-start.66 = (f32[8,64]{1,0:T(8,128)S(1)}, f32[8,64]{1,0:T(8,128)}, u32[]{:S(2)}) copy-start(f32[8,64]{1,0:T(8,128)} %copy-done.64) | copy-start | bytes 6148
  3226.4 502.8 %copy-start.76 = (f32[8,128]{1,0:T(8,128)S(1)}, f32[8,128]{1,0:T(8,128)}, u32[]{:S(2)}) copy-start(f32[8,128]{1,0:T(8,128)} %copy-done.75) | copy-start | bytes 12292
  3226.4 502.8 %copy-start.78 = (f32[8,128]{1,0:T(8,128)S(1)}, f32[8,128]{1,0:T(8,128)}, u32[]{:S(2)}) copy-start(f32[8,128]{1,0:T(8,128)} %copy-done.77) | copy-start | bytes 12292
  (114 other events, 453.6 us)
Sparse Core Ops, SparseCore 0:
  19.3 483.1 all-gather.5
  504.6 176.3 all-gather.3
  754.6 480.9 all-gather.7
  1732.1 403.7 reduce-scatter.39
  2139.1 61.5 reduce-scatter.47
  2486.2 61.5 reduce-scatter.43
  2551.0 61.4 reduce-scatter.37
  2616.2 61.4 reduce-scatter.35
  2681.2 63.7 reduce-scatter.33
  2748.5 61.3 reduce-scatter.31
  2813.8 61.3 reduce-scatter.29
  2879.4 63.8 reduce-scatter.27
  2947.1 60.0 reduce-scatter.45
  3010.6 206.3 reduce-scatter.25
  3220.7 60.2 reduce-scatter.41
  3284.8 36.2 all-reduce.3
  3325.3 403.8 reduce-scatter.23
where the time goes:
time: 3770 us; the launch traced here: 3740 us
  waiting for transfers between devices  1950 us (52%)
  matrix products  940 us (25%)
  local copies, waits for them, and re-layouts  551 us (15%)
  loops' own time  143 us (4%)
  other arithmetic  135 us (4%)
    all_gather x1, waiting for transfers between devices, enc_collect(): return lax.all_gather(pieces, 'seq', axis=1, tiled=True)  456 us
    reduce_scatter x1, waiting for transfers between devices, enc_spread(): lax.psum_scatter(pieces.astype(jnp.bfloat16), 'seq', scatter_dimension=1,...  396 us
    all_gather x1, waiting for transfers between devices, memory_collect(): return lax.all_gather(pieces, 'seq', axis=1, tiled=True)  284 us
    unnamed x22, waiting for transfers between devices  219 us
    reduce_scatter x1, waiting for transfers between devices, dec_spread(): lax.psum_scatter(pieces.astype(jnp.bfloat16), 'seq', scatter_dimension=1,...  208 us
    unnamed x200, local copies, waits for them, and re-layouts  178 us
    dot_general x72, matrix products, score_parts(): jnp.einsum('rqhe,rkhe->rhqk', query_heads, key_heads, preferred_element_t...  150 us
    dot_general x36, matrix products, attend_forward(): jnp.einsum('rhqk,rkhe->rqhe', (weights / row_total[..., None]).astype(jnp...  88.1 us
  transfers between devices with their start and end apart: 17, of which 14 were waited for; matrix products, arithmetic and copies ran while one was open for 31% of the time, Pallas kernels for 0%

commit v1 on v0

v1 whole, which is shorter than its diff:
```python
import functools
import math

import jax
import jax.numpy as jnp
from jax import lax
from jax.experimental import pallas as pl
from jax.experimental.pallas import tpu as pltpu
from jax.sharding import PartitionSpec as P

HEAD = 64
GROUP = 4
PAD = 32
BIG = 2.0**100
LOG2E = math.log2(math.e)
QUERY_SCALE = LOG2E / math.sqrt(HEAD)
VMEM_BYTES = 60 * 2**20
LOW = jnp.bfloat16
WIDE = jnp.float32


def contract(left, right, left_dim, right_dim):
    return lax.dot_general(
        left, right, (((left_dim,), (right_dim,)), ((), ())), preferred_element_type=WIDE
    )


def project(left, right):
    return jnp.dot(left, right, preferred_element_type=WIDE)


def project_wide(weight, rows):
    return jnp.einsum("io,ti->ot", weight, rows, preferred_element_type=WIDE)


def back_through(gradient, weight):
    return jnp.einsum("ln,dn->ld", gradient, weight, preferred_element_type=WIDE)


def weight_grad(inputs, gradient):
    return jnp.einsum("la,lb->ab", inputs, gradient, preferred_element_type=WIDE)


def normalize(value):
    centered = value - jnp.mean(value, axis=-1, keepdims=True)
    inverse = lax.rsqrt(jnp.mean(centered * centered, axis=-1, keepdims=True) + 1e-05)
    return (centered * inverse, inverse)


def normalize_back(gradient, normed, inverse):
    return (
        gradient
        - jnp.mean(gradient, axis=-1, keepdims=True)
        - normed * jnp.mean(gradient * normed, axis=-1, keepdims=True)
    ) * inverse


def gelu_act(value):
    return jax.nn.gelu(value, approximate=True)


def gelu_back(value, gradient):
    return jax.vjp(gelu_act, value)[1](gradient)[0]


def rows_at(head, size):
    return pl.ds(pl.multiple_of(head * size, size), size)


def split_three(value):
    high = value.astype(LOW).astype(WIDE)
    rest = value - high
    middle = rest.astype(LOW).astype(WIDE)
    return (high, middle, rest - middle)


def place_rows(parts, first, shape):
    row = lax.broadcasted_iota(jnp.int32, shape, 0)
    out = jnp.zeros(shape, WIDE)
    for offset, part in enumerate(parts):
        out = jnp.where(row == first + offset, part, out)
    return out


def document_rows(segments, shape, is_key):
    row = lax.broadcasted_iota(jnp.int32, shape, 0)
    same = row == segments
    if is_key:
        return jnp.where(row < 4, jnp.where(same, 0.0, -BIG), 0.0)
    return jnp.where(same & (row < 4), 1.0, 0.0)


def column_peak(scores, peak):
    for start in range(0, scores.shape[0], 8):
        peak = jnp.maximum(peak, scores[start : start + 8])
    return peak


def attend_kernel(tile, causal, prefix, *refs):
    if prefix:
        q_ref, k_ref, v_ref, qseg_ref, kseg_ref, pk_ref, pv_ref = refs[:7]
        refs = refs[7:]
    else:
        q_ref, k_ref, v_ref, qseg_ref, kseg_ref = refs[:5]
        refs = refs[5:]
    out_ref, lse_ref, qx_ref, kx_ref, s_ref, sp_ref, peak_ref = refs
    width, queries = q_ref.shape
    keys = k_ref.shape[1]
    heads = width // HEAD
    tiles = keys // tile
    qx_ref[...] = document_rows(qseg_ref[...], qx_ref.shape, False).astype(LOW)
    kx_ref[...] = document_rows(kseg_ref[...], kx_ref.shape, True).astype(LOW)
    start_peak = jnp.full((8, queries), -4.0 * BIG, WIDE)

    def query_of(head):
        return jnp.concatenate([q_ref[rows_at(head, HEAD), :], qx_ref[...]], 0)

    def tile_scores(head, part, query):
        cut = slice(part * tile, (part + 1) * tile)
        key = jnp.concatenate([k_ref[rows_at(head, HEAD), cut], kx_ref[:, cut]], 0)
        scores = contract(key, query, 0, 0)
        if causal:
            place = lax.broadcasted_iota(jnp.int32, scores.shape, 0) + part * tile
            scores = jnp.where(
                place <= lax.broadcasted_iota(jnp.int32, scores.shape, 1), scores, -BIG
            )
        return scores

    def prefix_scores(head, slot):
        if not prefix:
            return start_peak
        scores = contract(pk_ref[rows_at(head, HEAD), :], q_ref[rows_at(head, HEAD), :], 0, 0)
        row = lax.broadcasted_iota(jnp.int32, scores.shape, 0)
        scores = jnp.where(row < prefix, scores, -BIG)
        sp_ref[slot] = scores
        return column_peak(scores, start_peak)

    def score_tile(head, part, query, slot, peak):
        scores = tile_scores(head, part, query)
        s_ref[slot, part * tile : (part + 1) * tile, :] = scores
        return column_peak(scores, peak)

    def step(head, following, slot):
        other = 1 - slot
        query = query_of(following)
        peak = jnp.max(peak_ref[slot], 0, keepdims=True)
        next_peak = prefix_scores(following, other)
        context = jnp.zeros((HEAD + 16, queries), WIDE)
        if prefix:
            weights = jnp.exp2(sp_ref[slot] - peak).astype(LOW)
            value = jnp.concatenate(
                [pv_ref[rows_at(head, HEAD), :], jnp.ones((16, PAD), LOW)], 0
            )
            context = contract(value, weights, 1, 0)
        for part in range(tiles):
            next_peak = score_tile(following, part, query, other, next_peak)
            cut = slice(part * tile, (part + 1) * tile)
            weights = jnp.exp2(s_ref[slot, cut, :] - peak).astype(LOW)
            value = jnp.concatenate(
                [v_ref[rows_at(head, HEAD), cut], jnp.ones((16, tile), LOW)], 0
            )
            context = context + contract(value, weights, 1, 0)
        peak_ref[other] = next_peak
        total = context[HEAD : HEAD + 1]
        out_ref[rows_at(head, HEAD), :] = (context[:HEAD] * (1.0 / total)).astype(LOW)
        lse_ref[pl.ds(head, 1), :] = peak + jnp.log2(total)

    first = query_of(0)
    peak = prefix_scores(0, 0)
    for part in range(tiles):
        peak = score_tile(0, part, first, 0, peak)
    peak_ref[0] = peak

    def pair(index, carry):
        step(2 * index, 2 * index + 1, 0)
        step(2 * index + 1, jnp.minimum(2 * index + 2, heads - 1), 1)
        return carry

    lax.fori_loop(0, heads // 2, pair, 0)


def whole(shape):
    return pl.BlockSpec(shape, lambda step: (0,) * len(shape))


def third(width, tokens, index):
    return pl.BlockSpec((width, tokens), lambda step: (index, 0))


def attend(q_all, kv_all, places, q_segments, k_segments, prefix_pairs, causal):
    queries, keys = q_all.shape[1], kv_all.shape[1]
    width = q_all.shape[0] if places[0] == 0 and q_all is not kv_all else q_all.shape[0] // 3
    tile = min(256, keys)
    operands = [q_all, kv_all, kv_all, q_segments, k_segments]
    specs = [
        third(width, queries, places[0]),
        third(width, keys, places[1]),
        third(width, keys, places[2]),
        whole((1, queries)),
        whole((1, keys)),
    ]
    count = 0
    if prefix_pairs is not None:
        count = prefix_pairs.shape[0]
        padded = jnp.pad(prefix_pairs, ((0, PAD - count), (0, 0))).T
        operands += [padded, padded]
        specs += [third(width, PAD, 0), third(width, PAD, 1)]
    lse_rows = -(-(width // HEAD) // 8) * 8
    return pl.pallas_call(
        functools.partial(attend_kernel, tile, causal, count),
        grid=(1,),
        out_shape=(
            jax.ShapeDtypeStruct((width, queries), LOW),
            jax.ShapeDtypeStruct((lse_rows, queries), WIDE),
        ),
        in_specs=specs,
        out_specs=(whole((width, queries)), whole((lse_rows, queries))),
        scratch_shapes=[
            pltpu.VMEM((16, queries), LOW),
            pltpu.VMEM((16, keys), LOW),
            pltpu.VMEM((2, keys, queries), WIDE),
            pltpu.VMEM((2, PAD, queries), WIDE),
            pltpu.VMEM((2, 8, queries), WIDE),
        ],
        compiler_params=pltpu.CompilerParams(vmem_limit_bytes=VMEM_BYTES),
        name="attend",
    )(*operands)


def attend_back_kernel(tile, causal, prefix, *refs):
    q_ref, k_ref, v_ref, dc_ref, ctx_ref, lse_ref, qseg_ref, kseg_ref = refs[:8]
    refs = refs[8:]
    if prefix:
        pk_ref, pv_ref, dq_out, dk_out, dv_out, dpk_out, dpv_out = refs[:7]
        refs = refs[7:]
    else:
        dq_out, dk_out, dv_out = refs[:3]
        refs = refs[3:]
    qx_ref, kx_ref, dx_ref, vx_ref, delta_ref, dq_ref, p_ref, ds_ref = refs
    width, queries = q_ref.shape
    keys = k_ref.shape[1]
    heads = width // HEAD
    tiles = keys // tile
    scale = 1.0 / math.sqrt(HEAD)
    row = lax.broadcasted_iota(jnp.int32, (16, keys), 0)
    kx_ref[...] = jnp.where(
        (row >= 4) & (row < 7), 1.0, document_rows(kseg_ref[...], (16, keys), True)
    ).astype(LOW)
    vx_ref[...] = jnp.where(row < 3, 1.0, 0.0).astype(LOW)
    documents = document_rows(qseg_ref[...], (16, queries), False)

    def prepare(head, carry):
        delta = jnp.sum(
            dc_ref[rows_at(head, HEAD), :].astype(WIDE) * ctx_ref[rows_at(head, HEAD), :].astype(WIDE),
            axis=0,
            keepdims=True,
        )
        delta_ref[pl.ds(head, 1), :] = delta
        dx_ref[rows_at(head, 16), :] = place_rows(split_three(-delta), 0, (16, queries)).astype(LOW)
        minus = split_three(-lse_ref[pl.ds(head, 1), :])
        qx_ref[rows_at(head, 16), :] = (
            documents + place_rows(minus, 4, (16, queries))
        ).astype(LOW)
        return carry

    lax.fori_loop(0, heads, prepare, 0)

    if prefix:
        for group in range(heads // GROUP):
            wide = slice(group * GROUP * HEAD, (group + 1) * GROUP * HEAD)
            tall = slice(group * GROUP * PAD, (group + 1) * GROUP * PAD)
            scores = contract(pk_ref[tall, :], q_ref[wide, :], 1, 0)
            gains = contract(pv_ref[tall, :], dc_ref[wide, :], 1, 0)
            chances, changes = [], []
            for member in range(GROUP):
                head = group * GROUP + member
                part = slice(member * PAD, (member + 1) * PAD)
                chance = jnp.exp2(scores[part] - lse_ref[head : head + 1, :])
                place = lax.broadcasted_iota(jnp.int32, chance.shape, 0)
                chance = jnp.where(place < prefix, chance, 0.0)
                chances.append(chance.astype(LOW))
                changes.append((chance * (gains[part] - delta_ref[head : head + 1, :])).astype(LOW))
            chances = jnp.concatenate(chances, 0)
            changes = jnp.concatenate(changes, 0)
            dq_ref[wide, :] = contract(pk_ref[tall, :], changes, 0, 0)
            dpk_out[tall, :] = contract(changes, q_ref[wide, :], 1, 1) * (1.0 / LOG2E)
            dpv_out[tall, :] = contract(chances, dc_ref[wide, :], 1, 1)
    else:
        dq_ref[...] = jnp.zeros(dq_ref.shape, WIDE)

    def front(head, part, slot):
        cut = slice(part * tile, (part + 1) * tile)
        query = jnp.concatenate([q_ref[rows_at(head, HEAD), :], qx_ref[rows_at(head, 16), :]], 0)
        key = jnp.concatenate([k_ref[rows_at(head, HEAD), cut], kx_ref[:, cut]], 0)
        scores = contract(query, key, 0, 0)
        if causal:
            place = lax.broadcasted_iota(jnp.int32, scores.shape, 1) + part * tile
            scores = jnp.where(
                place <= lax.broadcasted_iota(jnp.int32, scores.shape, 0), scores, -BIG
            )
        grad = jnp.concatenate([dc_ref[rows_at(head, HEAD), :], dx_ref[rows_at(head, 16), :]], 0)
        value = jnp.concatenate([v_ref[rows_at(head, HEAD), cut], vx_ref[:, cut]], 0)
        gains = contract(grad, value, 0, 0)
        chance = jnp.exp2(scores)
        p_ref[slot] = chance.astype(LOW)
        ds_ref[slot] = (chance * gains).astype(LOW)

    def back(head, part, slot):
        cut = slice(part * tile, (part + 1) * tile)
        rows = rows_at(head, HEAD)
        dv_out[rows, cut] = contract(dc_ref[rows, :], p_ref[slot], 1, 0).astype(LOW)
        dk_out[rows, cut] = (contract(q_ref[rows, :], ds_ref[slot], 1, 0) * (1.0 / LOG2E)).astype(LOW)
        dq_ref[rows, :] += contract(k_ref[rows, cut], ds_ref[slot], 1, 1)

    def one_head(head, carry):
        for part in range(tiles):
            last = part == tiles - 1
            front(
                jnp.minimum(head + 1, heads - 1) if last else head,
                0 if last else part + 1,
                (part + 1) % 2,
            )
            back(head, part, part % 2)
        dq_out[rows_at(head, HEAD), :] = (dq_ref[rows_at(head, HEAD), :] * scale).astype(LOW)
        return carry

    front(0, 0, 0)
    lax.fori_loop(0, heads, one_head, 0)


def block_diagonal(pairs, width):
    count = pairs.shape[0]
    heads = width // HEAD
    padded = jnp.pad(pairs, ((0, PAD - count), (0, 0))).reshape(PAD, heads // GROUP, GROUP, HEAD)
    spread = jnp.einsum("pgae,ab->gapbe", padded, jnp.eye(GROUP, dtype=pairs.dtype))
    return spread.reshape(heads * PAD, GROUP * HEAD)


def from_block_diagonal(grads, count):
    rows, columns = grads.shape
    heads = rows // PAD
    spread = grads.reshape(heads // GROUP, GROUP, PAD, GROUP, HEAD)
    own = jnp.einsum("gapae->pgae", spread)
    return own.reshape(PAD, heads * HEAD)[:count]


def attend_back(
    q_all, kv_all, places, context_grad, context, row_lse, q_segments, k_segments, prefix_pairs, causal
):
    width, queries = context.shape
    keys = kv_all.shape[1]
    tile = min(256, keys // 2)
    lse_rows = row_lse.shape[0]
    heads = width // HEAD
    operands = [q_all, kv_all, kv_all, context_grad, context, row_lse, q_segments, k_segments]
    specs = [
        third(width, queries, places[0]),
        third(width, keys, places[1]),
        third(width, keys, places[2]),
        whole((width, queries)),
        whole((width, queries)),
        whole((lse_rows, queries)),
        whole((1, queries)),
        whole((1, keys)),
    ]
    outs = [
        jax.ShapeDtypeStruct((width, queries), LOW),
        jax.ShapeDtypeStruct((width, keys), LOW),
        jax.ShapeDtypeStruct((width, keys), LOW),
    ]
    count = 0
    if prefix_pairs is not None:
        count = prefix_pairs.shape[0]
        block = (heads * PAD, GROUP * HEAD)
        operands += [
            block_diagonal(prefix_pairs[:, :width], width),
            block_diagonal(prefix_pairs[:, width:], width),
        ]
        specs += [whole(block), whole(block)]
        outs += [jax.ShapeDtypeStruct(block, WIDE)] * 2
    results = pl.pallas_call(
        functools.partial(attend_back_kernel, tile, causal, count),
        grid=(1,),
        out_shape=tuple(outs),
        in_specs=specs,
        out_specs=tuple(whole(out.shape) for out in outs),
        scratch_shapes=[
            pltpu.VMEM((heads * 16, queries), LOW),
            pltpu.VMEM((16, keys), LOW),
            pltpu.VMEM((heads * 16, queries), LOW),
            pltpu.VMEM((16, keys), LOW),
            pltpu.VMEM((lse_rows, queries), WIDE),
            pltpu.VMEM((width, queries), WIDE),
            pltpu.VMEM((2, queries, tile), LOW),
            pltpu.VMEM((2, queries, tile), LOW),
        ],
        compiler_params=pltpu.CompilerParams(vmem_limit_bytes=VMEM_BYTES),
        name="attend_back",
    )(*operands)
    if prefix_pairs is None:
        return (results[0], results[1], results[2], None)
    pair_grad = jnp.concatenate(
        [from_block_diagonal(results[3], count), from_block_diagonal(results[4], count)], axis=1
    )
    return (results[0], results[1], results[2], pair_grad)


def prefix_forward(prefix, prefix_in, prefix_out):
    hidden = jnp.tanh(jnp.dot(prefix, prefix_in, preferred_element_type=WIDE))
    pair_rows = jnp.dot(hidden, prefix_out.astype(WIDE), precision=lax.Precision.HIGHEST)
    return (hidden, pair_rows.astype(LOW))


def prefix_backward(prefix, prefix_in, prefix_out, hidden, pair_grad, place, count):
    def share(value, axis):
        size = value.shape[axis] // count
        return lax.dynamic_slice_in_dim(value, place * size, size, axis).astype(WIDE)

    exact = functools.partial(jnp.matmul, precision=lax.Precision.HIGHEST)
    out_grad = exact(share(hidden, 1).T, pair_grad)
    hidden_grad = exact(pair_grad, prefix_out.astype(WIDE).T) * (1.0 - hidden * hidden)
    in_grad = exact(share(prefix, 1).T, hidden_grad)
    embed_grad = exact(hidden_grad, share(prefix_in, 0).T)
    return (embed_grad, in_grad, out_grad)


def scaled_queries(rows, width):
    row = lax.broadcasted_iota(jnp.int32, (rows.shape[0], 1), 0)
    return (rows * jnp.where(row < width, QUERY_SCALE, 1.0)).astype(LOW)


def self_forward(hidden, qkv_weight, out_weight, prefix_pairs, segments, causal):
    width = hidden.shape[1]
    qkv = scaled_queries(project_wide(qkv_weight, hidden), width)
    context, row_lse = attend(qkv, qkv, (0, 1, 2), segments, segments, prefix_pairs, causal)
    branch = jnp.einsum("it,io->to", context, out_weight, preferred_element_type=WIDE)
    normed, inverse = normalize(hidden.astype(WIDE) + branch)
    return (normed, (qkv, context, row_lse, normed, inverse))


def self_backward(gradient, stored, qkv_weight, out_weight, prefix_pairs, segments, causal):
    qkv, context, row_lse, normed, inverse = stored
    summed_grad = normalize_back(gradient, normed, inverse)
    context_grad = jnp.einsum(
        "io,to->it", out_weight, summed_grad.astype(LOW), preferred_element_type=WIDE
    ).astype(LOW)
    query_grad, key_grad, value_grad, pair_grad = attend_back(
        qkv, qkv, (0, 1, 2), context_grad, context, row_lse, segments, segments, prefix_pairs, causal
    )
    qkv_grad = jnp.concatenate([query_grad, key_grad, value_grad], axis=0)
    hidden_grad = summed_grad + jnp.einsum(
        "ot,io->ti", qkv_grad, qkv_weight, preferred_element_type=WIDE
    )
    return (hidden_grad, pair_grad)


def feed_forward(hidden, up_weight, down_weight, adapter_down, adapter_up):
    hidden_low = hidden.astype(LOW)
    inner_pre = project(hidden_low, up_weight)
    active = gelu_act(inner_pre).astype(LOW)
    narrow = project(hidden_low, adapter_down)
    narrow_act = gelu_act(narrow).astype(LOW)
    summed = hidden + project(active, down_weight) + 4.0 * project(narrow_act, adapter_up)
    normed, inverse = normalize(summed)
    return (normed, (hidden_low, inner_pre, narrow, narrow_act, normed, inverse))


def feed_backward(gradient, stored, up_weight, down_weight, adapter_down, adapter_up):
    hidden_low, inner_pre, narrow, narrow_act, normed, inverse = stored
    summed_grad = normalize_back(gradient, normed, inverse)
    main_grad = summed_grad.astype(LOW)
    side_grad = (4.0 * summed_grad).astype(LOW)
    adapter_up_grad = weight_grad(narrow_act, side_grad)
    narrow_grad = gelu_back(narrow, back_through(side_grad, adapter_up)).astype(LOW)
    adapter_down_grad = weight_grad(hidden_low, narrow_grad)
    inner_grad = gelu_back(inner_pre, back_through(main_grad, down_weight)).astype(LOW)
    hidden_grad = (
        summed_grad + back_through(inner_grad, up_weight) + back_through(narrow_grad, adapter_down)
    )
    return (hidden_grad, adapter_down_grad, adapter_up_grad)


def one_row(
    source,
    target,
    source_segments,
    target_segments,
    cotangent,
    weights,
    enc_pairs,
    dec_pairs,
):
    (
        enc_qkv,
        enc_out,
        enc_up,
        enc_down,
        dec_qkv,
        dec_out,
        cross_q,
        cross_kv,
        cross_out,
        dec_up,
        dec_down,
        enc_adapter_down,
        enc_adapter_up,
        dec_adapter_down,
        dec_adapter_up,
    ) = weights
    width = source.shape[1]
    encoded_mid, encoded_stored = self_forward(
        source, enc_qkv, enc_out, enc_pairs, source_segments, False
    )
    memory, memory_stored = feed_forward(
        encoded_mid, enc_up, enc_down, enc_adapter_down, enc_adapter_up
    )
    decoded_mid, decoded_stored = self_forward(
        target, dec_qkv, dec_out, dec_pairs, target_segments, True
    )
    cross_query = scaled_queries(project_wide(cross_q, decoded_mid.astype(LOW)), width)
    memory_pairs = project_wide(cross_kv, memory.astype(LOW)).astype(LOW)
    cross_context, cross_lse = attend(
        cross_query, memory_pairs, (0, 0, 1), target_segments, source_segments, None, False
    )
    crossed, crossed_inverse = normalize(
        decoded_mid
        + jnp.einsum("it,io->to", cross_context, cross_out, preferred_element_type=WIDE)
    )
    output_wide, output_stored = feed_forward(
        crossed, dec_up, dec_down, dec_adapter_down, dec_adapter_up
    )
    crossed_grad, dec_adapter_down_grad, dec_adapter_up_grad = feed_backward(
        cotangent.astype(WIDE), output_stored, dec_up, dec_down, dec_adapter_down, dec_adapter_up
    )
    cross_sum_grad = normalize_back(crossed_grad, crossed, crossed_inverse)
    context_grad = jnp.einsum(
        "io,to->it", cross_out, cross_sum_grad.astype(LOW), preferred_element_type=WIDE
    ).astype(LOW)
    query_grad, key_grad, value_grad, _ = attend_back(
        cross_query,
        memory_pairs,
        (0, 0, 1),
        context_grad,
        cross_context,
        cross_lse,
        target_segments,
        source_segments,
        None,
        False,
    )
    pair_grad = jnp.concatenate([key_grad, value_grad], axis=0)
    memory_grad = jnp.einsum("ot,io->ti", pair_grad, cross_kv, preferred_element_type=WIDE)
    decoded_grad = cross_sum_grad + jnp.einsum(
        "ot,io->ti", query_grad, cross_q, preferred_element_type=WIDE
    )
    target_grad, dec_pair_grad = self_backward(
        decoded_grad, decoded_stored, dec_qkv, dec_out, dec_pairs, target_segments, True
    )
    encoded_grad, enc_adapter_down_grad, enc_adapter_up_grad = feed_backward(
        memory_grad, memory_stored, enc_up, enc_down, enc_adapter_down, enc_adapter_up
    )
    source_grad, enc_pair_grad = self_backward(
        encoded_grad, encoded_stored, enc_qkv, enc_out, enc_pairs, source_segments, False
    )
    activations = (output_wide.astype(LOW), source_grad.astype(LOW), target_grad.astype(LOW))
    adapter_grads = (
        enc_adapter_down_grad,
        enc_adapter_up_grad,
        dec_adapter_down_grad,
        dec_adapter_up_grad,
    )
    return (activations, adapter_grads, (enc_pair_grad, dec_pair_grad))


def total(values):
    return functools.reduce(lambda left, right: left + right, values)


def shards(
    source,
    target,
    source_segments,
    target_segments,
    cotangent,
    enc_qkv,
    enc_out,
    enc_up,
    enc_down,
    dec_qkv,
    dec_out,
    cross_q,
    cross_kv,
    cross_out,
    dec_up,
    dec_down,
    enc_prefix,
    enc_prefix_in,
    enc_prefix_out,
    enc_adapter_down,
    enc_adapter_up,
    dec_prefix,
    dec_prefix_in,
    dec_prefix_out,
    dec_adapter_down,
    dec_adapter_up,
    *,
    count,
):
    place = lax.axis_index("seq")
    rows = source.shape[0]
    copies = max(count // rows, 1)
    own = max(rows // count, 1)

    def bring(value):
        return lax.all_to_all(jnp.repeat(value, copies, axis=0), "seq", 0, 1, tiled=True)

    def send_back(value):
        return lax.all_to_all(value, "seq", 1, 0, tiled=True)[::copies]

    def own_rows(segments):
        return lax.dynamic_slice_in_dim(segments, place // copies * own, own, 0)

    source_rows, target_rows, cotangent_rows = bring(source), bring(target), bring(cotangent)
    source_marks, target_marks = own_rows(source_segments), own_rows(target_segments)
    enc_hidden, enc_pairs = prefix_forward(enc_prefix, enc_prefix_in, enc_prefix_out)
    dec_hidden, dec_pairs = prefix_forward(dec_prefix, dec_prefix_in, dec_prefix_out)
    weights = (
        enc_qkv,
        enc_out,
        enc_up,
        enc_down,
        dec_qkv,
        dec_out,
        cross_q,
        cross_kv,
        cross_out,
        dec_up,
        dec_down,
        enc_adapter_down,
        enc_adapter_up,
        dec_adapter_down,
        dec_adapter_up,
    )
    results = [
        one_row(
            source_rows[row],
            target_rows[row],
            source_marks[row : row + 1],
            target_marks[row : row + 1],
            cotangent_rows[row],
            weights,
            enc_pairs,
            dec_pairs,
        )
        for row in range(own)
    ]
    activations = [send_back(jnp.stack(parts)) for parts in zip(*(result[0] for result in results))]
    share = 1.0 / copies
    adapters = [total(parts) * share for parts in zip(*(result[1] for result in results))]
    adapters = [
        lax.psum(
            lax.psum_scatter(grad.astype(LOW), "seq", scatter_dimension=0, tiled=True), "dp"
        ).astype(WIDE)
        for grad in adapters
    ]
    pair_grads = [total(parts) * share for parts in zip(*(result[2] for result in results))]
    enc_pair_grad, dec_pair_grad = lax.psum(tuple(pair_grads), ("dp", "seq"))
    enc_prefix_grads = prefix_backward(
        enc_prefix, enc_prefix_in, enc_prefix_out, enc_hidden, enc_pair_grad, place, count
    )
    dec_prefix_grads = prefix_backward(
        dec_prefix, dec_prefix_in, dec_prefix_out, dec_hidden, dec_pair_grad, place, count
    )
    return (
        activations[0],
        activations[1].astype(WIDE),
        activations[2].astype(WIDE),
        *enc_prefix_grads,
        adapters[0],
        adapters[1],
        *dec_prefix_grads,
        adapters[2],
        adapters[3],
    )


def solution(mesh):
    rows = P("dp", "seq", None)
    marks = P("dp", None)
    in_specs = (rows, rows, marks, marks, rows) + (P(),) * 21
    across, down = P(None, "seq"), P("seq", None)
    layer = (across, down, down, down, down)
    return jax.shard_map(
        functools.partial(shards, count=mesh.shape["seq"]),
        mesh=mesh,
        in_specs=in_specs,
        out_specs=(rows, rows, rows) + layer + layer,
        check_vma=False,
    )
```

time: 3770 us -> 725 us (0.19)
  waiting for transfers between devices: 1950 us -> 204 us
  matrix products: 940 us -> 186 us
  local copies, waits for them, and re-layouts: 551 us -> 113 us
  loops' own time: 143 us -> 0 us
  Pallas kernels: 0 us -> 112 us
  other arithmetic: 135 us -> 54 us
    reduce_scatter x8 -> x4, waiting for transfers between devices: 963 us -> 125 us  [shards(): lax.psum_scatter(grad.astype(LOW), 'seq', scatter_dimension=0, tiled=True)]
    dot_general x464 -> x44, matrix products: 940 us -> 186 us  [the longest x6 51.9 us: back_through(): jnp.einsum('ln,dn->ld', gradient, weight, preferred_element_type=WIDE)]
    all_gather x3 -> x0, waiting for transfers between devices: 740 us -> none  [the longest x1 456 us: enc_collect(): return lax.all_gather(pieces, 'seq', axis=1, tiled=True)]
    unnamed x22 -> x6, waiting for transfers between devices: 219 us -> 0.1 us
    another operation x6 -> x0, loops' own time: 143 us -> none  [the longest x3 71.7 us: attend_backward_blocks(): lax.map(one_head, jnp.arange(query_heads.shape[2]))]
    unnamed x200 -> x142, local copies, waits for them, and re-layouts: 178 us -> 46.8 us
    slice x16 -> x14, local copies, waits for them, and re-layouts: 141 us -> 13.8 us  [the longest x12 12.4 us: from_block_diagonal(): return own.reshape(PAD, heads * HEAD)[:count]]
    pallas_call x0 -> x6, Pallas kernels: none -> 112 us  [the longest x3 77 us: attend_back(): pl.pallas_call(functools.partial(attend_back_kernel, tile, causal, count)...]
  transfers between devices with their start and end apart: 17 -> 12, of which waited for: 14 -> 8; matrix products, arithmetic and copies ran while one was open for 31% -> 24% of each run, Pallas kernels for 0% -> 1%
where the time goes in v1:
time: 725 us; the launch traced here: 717 us
  waiting for transfers between devices  204 us (28%)
  matrix products  186 us (26%)
  local copies, waits for them, and re-layouts  113 us (16%)
  Pallas kernels  112 us (15%)
  other arithmetic  54 us (7%)
  starting transfers between devices  31.2 us (4%)
  between operations  16.8 us (2%)
    reduce_scatter x4, waiting for transfers between devices, shards(): lax.psum_scatter(grad.astype(LOW), 'seq', scatter_dimension=0, tiled=True)  125 us
    pallas_call x3, Pallas kernels, attend_back(): pl.pallas_call(functools.partial(attend_back_kernel, tile, causal, count)...  77 us
    dot_general x6, matrix products, back_through(): jnp.einsum('ln,dn->ld', gradient, weight, preferred_element_type=WIDE)  51.9 us
    unnamed x142, local copies, waits for them, and re-layouts  46.8 us
    psum x1, waiting for transfers between devices, shards(): enc_pair_grad, dec_pair_grad = lax.psum(tuple(pair_grads), ('dp', 'seq'))  45.7 us
    pallas_call x3, Pallas kernels, attend(): pl.pallas_call(functools.partial(attend_kernel, tile, causal, count), gri...  34.5 us
    dot_general x8, matrix products, project(): return jnp.dot(left, right, preferred_element_type=WIDE)  33 us
    unnamed x6, other arithmetic  27 us
  transfers between devices with their start and end apart: 12, of which 8 were waited for; matrix products, arithmetic and copies ran while one was open for 24% of the time, Pallas kernels for 1%

profile of v1, /device:TPU:0, one launch (start us, length us, event | category | flops | bytes accessed | tf_op | source)
XLA Modules:
  0.0 717.0 jit_solution(17350401180380382504)
XLA Ops:
  8.0 7.5 %all-to-all-start = ((bf16[8,64,768]{2,1,0:T(8,128)(2,1)}), bf16[8,64,768]{2,1,0:T(8,128)(2,1)}, u32[]{:S(2)}, u32[]{:S(2)}) async-start(bf16[8,64,768]{2,1,0:T(8,128)(2,1)} %param.27), calls=%async_computation | async-start | bytes 1572864 | tf_op jit(solution)/shard_map/all_to_all | solution.py:615
  27.3 8.5 %all-to-all-done = bf16[8,64,768]{2,1,0:T(8,128)(2,1)} async-done(((bf16[8,64,768]{2,1,0:T(8,128)(2,1)}), bf16[8,64,768]{2,1,0:T(8,128)(2,1)}, u32[]{:S(2)}, u32[]{:S(2)}) %all-to-all-start) | async-done | bytes 786464 | tf_op jit(solution)/shard_map/all_to_all | solution.py:615
  84.5 7.1 attend.3
  103.3 7.6 %multiply_convert_fusion.1.refs_0_.refs_1_.refs_2_ = bf16[2304,1024]{1,0:T(8,128)(2,1)} fusion(bf16[768,2304]{1,0:T(8,128)(2,1)S(1)} %copy-done, bf16[1024,768]{1,0:T(8,128)(2,1)} %bitcast.3, f32[2304]{0:T(1024)S(1)} %fusion.106), kind=kOutput, calls=%fused_computation.10 | convolution fusion | flops 3628597248 | bytes 9839616 | tf_op jit(solution)/shard_map/io,ti->ot/dot_general | solution.py:33
  110.9 17.1 %attend.4 = (bf16[768,1024]{1,0:T(8,128)(2,1)}, f32[16,1024]{1,0:T(8,128)}) custom-call(bf16[2304,1024]{1,0:T(8,128)(2,1)} %multiply_convert_fusion.1.refs_0_.refs_1_.refs_2_, bf16[2304,1024]{1,0:T(8,128)(2,1)} %multiply_convert_fusion.1.refs_0_.refs_1_.refs_2_, bf16[2304,1024]{1,0:T(8,128)(2,1)} %multiply_convert_fusion.1.refs_0_.refs_1_.refs_2_, ...), custom_call_target="tpu_custom_call" | custom-call | tf_op jit(solution)/shard_map/attend/pallas_call | solution.py:209
  142.4 13.3 %fusion.14 = f32[1024,768]{0,1:T(8,128)} fusion(bf16[3072,768]{1,0:T(8,128)(2,1)} %param.34, f32[1024,3072]{1,0:T(8,128)S(1)} %fusion.157), kind=kOutput, calls=%fused_computation.21 | convolution fusion | flops 4860149760 | bytes 20447232 | tf_op jit(solution)/shard_map/dot_general | solution.py:29
  166.9 10.2 %attend.5 = (bf16[768,512]{1,0:T(8,128)(2,1)}, f32[16,512]{1,0:T(8,128)}) custom-call(bf16[768,512]{1,0:T(8,128)(2,1)} %fusion.68.refs_0_, bf16[1536,1024]{1,0:T(8,128)(2,1)} %fusion.24.refs_1_.refs_2_, bf16[1536,1024]{1,0:T(8,128)(2,1)} %fusion.24.refs_1_.refs_2_, s32[1,512]{1,0:T(1,128)} %constant_dynamic-slice_fusion.1.refs_3_.refs_4_.refs_6_.refs_7_, ...), custom_call_target="tpu_custom_call" | custom-call | tf_op jit(solution)/shard_map/attend/pallas_call | solution.py:209
  196.4 14.2 %fusion.30 = f32[512,768]{1,0:T(8,128)} fusion(bf16[768,3072]{1,0:T(8,128)(2,1)} %param.40, f32[512,3072]{1,0:T(8,128)} %copy-done.9, bf16[3072,768]{1,0:T(8,128)(2,1)} %param.41, f32[512,768]{1,0:T(8,128)} %copy-done.12), kind=kOutput, calls=%fused_computation.49 | convolution fusion | flops 4863688704 | bytes 18874368 | tf_op jit(solution)/shard_map/ln,dn->ld/dot_general | solution.py:37
  216.5 21.6 %attend_back.3 = (bf16[768,512]{1,0:T(8,128)(2,1)}, bf16[768,1024]{1,0:T(8,128)(2,1)}, bf16[768,1024]{1,0:T(8,128)(2,1)}) custom-call(bf16[768,512]{1,0:T(8,128)(2,1)} %fusion.68.refs_0_, bf16[1536,1024]{1,0:T(8,128)(2,1)} %fusion.24.refs_1_.refs_2_, bf16[1536,1024]{1,0:T(8,128)(2,1)} %fusion.24.refs_1_.refs_2_, bf16[768,512]{1,0:T(8,128)(2,1)} %fusion.69.refs_3_, ...), custom_call_target="tpu_custom_call" | custom-call | tf_op jit(solution)/shard_map/attend_back/pallas_call | solution.py:381
  238.1 6.3 fusion.147
  254.5 15.0 %attend_back.5 = (bf16[768,512]{1,0:T(8,128)(2,1)}, bf16[768,512]{1,0:T(8,128)(2,1)}, bf16[768,512]{1,0:T(8,128)(2,1)}, f32[384,256]{1,0:T(8,128)}, f32[384,256]{1,0:T(8,128)}) custom-call(bf16[2304,512]{1,0:T(8,128)(2,1)} %fusion.23.refs_0_.refs_1_.refs_2_, bf16[2304,512]{1,0:T(8,128)(2,1)} %fusion.23.refs_0_.refs_1_.refs_2_, ...), custom_call_target="tpu_custom_call" | custom-call | tf_op jit(solution)/shard_map/attend_back/pallas_call | solution.py:381
  278.0 24.6 %fusion.146 = (f32[1024]{0:T(1024)S(1)}, f32[1024]{0:T(1024)}, f32[1024,768]{0,1:T(8,128)}) fusion(f32[1024]{0:T(1024)S(1)} %add_rsqrt_fusion.1, f32[1024,768]{0,1:T(8,128)} %copy-done.4, f32[1024]{0:T(1024)S(1)} %broadcast_multiply_fusion.6, f32[1024,768]{0,1:T(8,128)} %fusion.161, f32[1024,768]{0,1:T(8,128)} %copy-done.21, bf16[768,3072]{1,0:T(8,128)(2,1)} %param.33, ...), kind=kOutput, calls=%fused_computation.226 | convolution fusion | flops 9732880384 | bytes 34619392 | tf_op jit(solution)/shard_map/ln,dn->ld/dot_general | solution.py:37
  309.1 40.3 %attend_back.4 = (bf16[768,1024]{1,0:T(8,128)(2,1)}, bf16[768,1024]{1,0:T(8,128)(2,1)}, bf16[768,1024]{1,0:T(8,128)(2,1)}, f32[384,256]{1,0:T(8,128)}, f32[384,256]{1,0:T(8,128)}) custom-call(bf16[2304,1024]{1,0:T(8,128)(2,1)} %multiply_convert_fusion.1.refs_0_.refs_1_.refs_2_, bf16[2304,1024]{1,0:T(8,128)(2,1)} %multiply_convert_fusion.1.refs_0_.refs_1_.refs_2_, ...), custom_call_target="tpu_custom_call" | custom-call | tf_op jit(solution)/shard_map/attend_back/pallas_call | solution.py:381
  376.3 6.0 fusion.71
  385.2 7.3 %reduce.6 = bf16[512,768]{1,0:T(8,128)(2,1)} reduce(bf16[512,1,768]{2,1,0:T(2,128)(2,1)} %bitcast.138, bf16[]{:T(256)} %broadcast.446), dimensions={1}, to_apply=%bitcast.134.reduce_sub_computation | reduce | bytes 1572866
  406.9 7.3 %reduce.4 = bf16[512,768]{1,0:T(8,128)(2,1)} reduce(bf16[512,1,768]{2,1,0:T(2,128)(2,1)} %bitcast.139, bf16[]{:T(256)} %broadcast.446), dimensions={1}, to_apply=%bitcast.135.reduce_sub_computation | reduce | bytes 1572866
  430.2 9.5 %fusion.60 = bf16[1,1024,768]{1,2,0:T(8,128)(2,1)} fusion(bf16[768,2304]{1,0:T(8,128)(2,1)S(1)} %copy-done, bf16[768,1024]{1,0:T(8,128)(2,1)} %get-tuple-element.41, bf16[768,1024]{1,0:T(8,128)(2,1)} %get-tuple-element.40, bf16[768,1024]{1,0:T(8,128)(2,1)} %get-tuple-element.39, f32[1024]{0:T(1024)S(1)} %copy-done.50, f32[1024]{0:T(1024)S(1)} %add_rsqrt_fusion.1, ...), kind=kOutput, calls=%fused_computation.99 | convolution fusion | flops 3644325888 | bytes 16138240 | tf_op jit(solution)/shard_map/ot,io->ti/dot_general | solution.py:451
  439.7 8.5 %copy.96 = bf16[1,1024,768]{2,0,1:T(2,128)(2,1)} copy(bf16[1,1024,768]{1,2,0:T(8,128)(2,1)} %fusion.60) | data formatting | bytes 3145728 | tf_op jit(solution)/shard_map/stack | solution.py:657
  448.3 12.4 %reduce.5 = bf16[1024,768]{1,0:T(8,128)(2,1)} reduce(bf16[1024,1,768]{2,1,0:T(2,128)(2,1)} %bitcast.136, bf16[]{:T(256)} %broadcast.446), dimensions={1}, to_apply=%bitcast.58.reduce_sub_computation | reduce | bytes 3145730
  474.2 45.7 %all-reduce.11.cloned.1.call-done = (f32[30,1536]{1,0:T(8,128)}, f32[30,1536]{1,0:T(8,128)}) async-done(((f32[30,1536]{1,0:T(8,128)}, f32[30,1536]{1,0:T(8,128)}), (f32[30,1536]{1,0:T(8,128)}, f32[30,1536]{1,0:T(8,128)})) %all-reduce.11.cloned.1.call-update) | async-done | bytes 368656 | tf_op jit(solution)/shard_map/psum | solution.py:667
  533.0 59.7 %reduce-scatter.7.cloned.1.call-done = bf16[64,768]{1,0:T(8,128)(2,1)} async-done(((bf16[512,768]{1,0:T(8,128)(2,1)}), bf16[64,768]{1,0:T(8,128)(2,1)}) %reduce-scatter.7.cloned.1.call-update) | async-done | bytes 98320 | tf_op jit(solution)/shard_map/reduce_scatter | solution.py:662
  592.7 65.5 %reduce-scatter.5.cloned.1.call-done = bf16[96,512]{1,0:T(8,128)(2,1)} async-done(((bf16[768,512]{1,0:T(8,128)(2,1)}), bf16[96,512]{1,0:T(8,128)(2,1)}) %reduce-scatter.5.cloned.1.call-update) | async-done | bytes 98320 | tf_op jit(solution)/shard_map/reduce_scatter | solution.py:662
  676.0 16.7 %all-reduce.13.cloned.1.call-done = (bf16[96,512]{1,0:T(8,128)(2,1)}, bf16[64,768]{1,0:T(8,128)(2,1)}, bf16[96,512]{1,0:T(8,128)(2,1)}, bf16[64,768]{1,0:T(8,128)(2,1)}) async-done(((bf16[96,512]{1,0:T(8,128)(2,1)}, bf16[64,768]{1,0:T(8,128)(2,1)}, bf16[96,512]{1,0:T(8,128)(2,1)}, bf16[64,768]{1,0:T(8,128)(2,1)}), (bf16[96,512]{1,0:T(8,128)(2,1)}, bf16[64,768]{1,0:T(8,128)(2,1)}, bf16[96,512]{1,0:T(8,128)(2,1)}, ...) | async-done | bytes 393232 | tf_op jit(solution)/shard_map/psum | solution.py:661
  699.1 6.4 reshape.249
  (285 shorter events, 261.8 us)
Async XLA Ops:
  8.0 95.3 %copy-start = (bf16[768,2304]{1,0:T(8,128)(2,1)S(1)}, bf16[768,2304]{1,0:T(8,128)(2,1)}, u32[]{:S(2)}) copy-start(bf16[768,2304]{1,0:T(8,128)(2,1)} %param.31) | copy-start | bytes 10616836
  8.0 27.8 %all-to-all-start = ((bf16[8,64,768]{2,1,0:T(8,128)(2,1)}), bf16[8,64,768]{2,1,0:T(8,128)(2,1)}, u32[]{:S(2)}, u32[]{:S(2)}) async-start(bf16[8,64,768]{2,1,0:T(8,128)(2,1)} %param.27), calls=%async_computation | async-start | bytes 1572864 | tf_op jit(solution)/shard_map/all_to_all | solution.py:615
  35.8 24.1 %all-to-all-start.3 = ((bf16[8,64,768]{2,1,0:T(8,128)(2,1)}), bf16[8,64,768]{2,1,0:T(8,128)(2,1)}, u32[]{:S(2)}, u32[]{:S(2)}) async-start(bf16[8,64,768]{2,1,0:T(8,128)(2,1)} %param.30), calls=%async_computation.3 | async-start | bytes 1572864 | tf_op jit(solution)/shard_map/all_to_all | solution.py:615
  59.9 40.8 %all-to-all-start.1 = ((bf16[8,128,768]{2,1,0:T(8,128)(2,1)}), bf16[8,128,768]{2,1,0:T(8,128)(2,1)}, u32[]{:S(2)}, u32[]{:S(2)}) async-start(bf16[8,128,768]{2,1,0:T(8,128)(2,1)} %param.26), calls=%async_computation.1 | async-start | bytes 3145728 | tf_op jit(solution)/shard_map/all_to_all | solution.py:615
  64.2 455.6 %all-reduce.11.cloned.1.call-start = ((), (), s32[]{:S(2)}) async-start(), calls=%async_computation.14 | async-start | bytes 786432 | tf_op jit(solution)/shard_map/psum | solution.py:667
  94.3 82.8 %copy-start.39 = (f32[512]{0:T(512)}, f32[512]{0:T(512)S(1)}, u32[]{:S(2)}) copy-start(f32[512]{0:T(512)S(1)} %broadcast_multiply_fusion.14) | copy-start | bytes 6148
  131.8 23.9 %copy-start.4 = (f32[1024,768]{0,1:T(8,128)}, f32[1024,768]{0,1:T(8,128)S(1)}, u32[]{:S(2)}) copy-start(f32[1024,768]{0,1:T(8,128)S(1)} %get-tuple-element.108) | copy-start | bytes 9437188
  142.4 13.3 %copy-start.7 = (f32[1024,3072]{1,0:T(8,128)}, f32[1024,3072]{1,0:T(8,128)S(1)}, u32[]{:S(2)}) copy-start(f32[1024,3072]{1,0:T(8,128)S(1)} %fusion.157) | copy-start | bytes 37748740
  142.4 13.3 %copy-start.26 = (bf16[512,768]{1,0:T(8,128)(2,1)S(1)}, bf16[512,768]{1,0:T(8,128)(2,1)}, u32[]{:S(2)}) copy-start(bf16[512,768]{1,0:T(8,128)(2,1)} %param.46) | copy-start | bytes 2359300
  160.0 6.9 copy-start.37
  166.9 10.3 %copy-start.46 = (f32[512]{0:T(512)S(1)}, f32[512]{0:T(512)}, u32[]{:S(2)}) copy-start(f32[512]{0:T(512)} %copy-done.45) | copy-start | bytes 6148
  180.2 7.7 %copy-start.1 = (f32[512,768]{1,0:T(8,128)}, f32[512,768]{1,0:T(8,128)S(1)}, u32[]{:S(2)}) copy-start(f32[512,768]{1,0:T(8,128)S(1)} %get-tuple-element.112) | copy-start | bytes 4718596
  184.1 9.2 %copy-start.17 = (f32[512,512]{1,0:T(8,128)}, f32[512,512]{1,0:T(8,128)S(1)}, u32[]{:S(2)}) copy-start(f32[512,512]{1,0:T(8,128)S(1)} %fusion.160) | copy-start | bytes 3145732
  216.5 21.7 %copy-start.38 = (f32[1024]{0:T(1024)S(1)}, f32[1024]{0:T(1024)}, u32[]{:S(2)}) copy-start(f32[1024]{0:T(1024)} %copy-done.37) | copy-start | bytes 12292
  216.5 21.7 %copy-start.43 = (f32[1024]{0:T(1024)S(1)}, f32[1024]{0:T(1024)}, u32[]{:S(2)}) copy-start(f32[1024]{0:T(1024)} %copy-done.42) | copy-start | bytes 12292
  373.4 159.6 %reduce-scatter.9.cloned.1.call-start = ((), (), s32[]{:S(2)}) async-start(), calls=%async_computation.12 | async-start | bytes 884736 | tf_op jit(solution)/shard_map/reduce_scatter | solution.py:662
  395.5 25.3 %all-to-all-start.5 = ((bf16[8,2,24576]{2,1,0:T(2,128)(2,1)}), bf16[8,2,24576]{2,1,0:T(2,128)(2,1)}, u32[]{:S(2)}, u32[]{:S(2)}) async-start(bf16[8,2,24576]{2,1,0:T(2,128)(2,1)} %reshape.250), calls=%async_computation.5 | async-start | bytes 1572864 | tf_op jit(solution)/shard_map/all_to_all | solution.py:618
  399.7 133.3 %reduce-scatter.11.cloned.1.call-start = ((), (), s32[]{:S(2)}) async-start(), calls=%async_computation.13 | async-start | bytes 884736 | tf_op jit(solution)/shard_map/reduce_scatter | solution.py:662
  420.8 43.6 %all-to-all-start.2 = ((bf16[8,2,24576]{2,1,0:T(2,128)(2,1)}), bf16[8,2,24576]{2,1,0:T(2,128)(2,1)}, u32[]{:S(2)}, u32[]{:S(2)}) async-start(bf16[8,2,24576]{2,1,0:T(2,128)(2,1)} %reshape.252), calls=%async_computation.2 | async-start | bytes 1572864 | tf_op jit(solution)/shard_map/all_to_all | solution.py:618
  425.0 167.7 %reduce-scatter.7.cloned.1.call-start = ((), (), s32[]{:S(2)}) async-start(), calls=%async_computation.11 | async-start | bytes 884736 | tf_op jit(solution)/shard_map/reduce_scatter | solution.py:662
  464.4 234.7 %all-to-all-start.4 = ((bf16[8,2,49152]{2,1,0:T(2,128)(2,1)}), bf16[8,2,49152]{2,1,0:T(2,128)(2,1)}, u32[]{:S(2)}, u32[]{:S(2)}) async-start(bf16[8,2,49152]{2,1,0:T(2,128)(2,1)} %reshape.248), calls=%async_computation.4 | async-start | bytes 3145728 | tf_op jit(solution)/shard_map/all_to_all | solution.py:618
  470.3 187.9 %reduce-scatter.5.cloned.1.call-start = ((), (), s32[]{:S(2)}) async-start(), calls=%async_computation.10 | async-start | bytes 884736 | tf_op jit(solution)/shard_map/reduce_scatter | solution.py:662
  473.9 218.8 %all-reduce.13.cloned.1.call-start = ((), (), s32[]{:S(2)}) async-start(), calls=%async_computation.15 | async-start | bytes 786432 | tf_op jit(solution)/shard_map/psum | solution.py:661
  519.9 9.7 %copy-start.30 = (f32[30,1536]{1,0:T(8,128)S(1)}, f32[30,1536]{1,0:T(8,128)}, u32[]{:S(2)}) copy-start(f32[30,1536]{1,0:T(8,128)} %get-tuple-element.90) | copy-start | bytes 552964
  (54 other events, 191.5 us)
Sparse Core Ops, SparseCore 0:
  373.6 146.2 all-reduce.10
Sparse Core Ops, SparseCore 1:
  377.6 69.3 reduce-scatter.8
  450.1 77.3 reduce-scatter.10
  531.0 61.6 reduce-scatter.6
  596.6 61.5 reduce-scatter.4
  660.9 31.7 all-reduce.12

commit v2 on v1

v2 whole, which is shorter than its diff:
```python
import functools
import math
from types import SimpleNamespace

import jax
import jax.numpy as jnp
from jax import lax
from jax.experimental import pallas as pl
from jax.experimental.pallas import tpu as pltpu
from jax.sharding import PartitionSpec as P

HEAD = 64
GROUP = 4
PAD = 32
BIG = 2.0**100
LOG2E = math.log2(math.e)
SCALE = 1.0 / math.sqrt(HEAD)
VMEM_BYTES = 60 * 2**20
CHUNK = 256
INNER = 512
LOW = jnp.bfloat16
WIDE = jnp.float32


def contract(left, right, left_dim, right_dim):
    return lax.dot_general(
        left, right, (((left_dim,), (right_dim,)), ((), ())), preferred_element_type=WIDE
    )


def rows_at(index, size, base=0):
    return pl.ds(pl.multiple_of(base + index * size, size), size)


def chunks(size, step):
    step = min(step, size)
    return [slice(start, start + step) for start in range(0, size, step)]


def normalize(value):
    centered = value - jnp.mean(value, axis=-1, keepdims=True)
    inverse = lax.rsqrt(jnp.mean(centered * centered, axis=-1, keepdims=True) + 1e-05)
    return (centered * inverse, inverse)


def normalize_back(gradient, normed, inverse):
    return (
        gradient
        - jnp.mean(gradient, axis=-1, keepdims=True)
        - normed * jnp.mean(gradient * normed, axis=-1, keepdims=True)
    ) * inverse


def gelu_both(value):
    scale = math.sqrt(2.0 / math.pi)
    square = value * value
    half = 0.5 + 0.5 * jnp.tanh(value * (scale + (scale * 0.044715) * square))
    active = value * half
    slope = half + active * (1.0 - half) * (2.0 * scale + (6.0 * scale * 0.044715) * square)
    return (active, slope)


class Mover:
    def __init__(self, semaphores):
        self.semaphores = semaphores
        self.used = 0

    def start(self, origin, goal):
        copy = pltpu.make_async_copy(origin, goal, self.semaphores.at[self.used])
        self.used += 1
        copy.start()
        return copy


def run_kernel(body, name, near, far, near_outs, far_outs, scratch, flops, links=0, collective=None):
    in_names = list(near) + list(far)
    out_names = list(near_outs) + list(far_outs)
    names = in_names + out_names + list(scratch) + ["semaphores"]
    link_scratch = []
    remote = {}
    if collective is not None:
        names += ["sent", "arrived"]
        link_scratch = [pltpu.SemaphoreType.DMA((links,)), pltpu.SemaphoreType.DMA((links,))]
        remote = dict(collective_id=collective, has_side_effects=True)

    def kernel(*refs):
        body(SimpleNamespace(**dict(zip(names, refs))))

    near_spec = pl.BlockSpec(memory_space=pltpu.VMEM)
    far_spec = pl.BlockSpec(memory_space=pl.ANY)
    results = pl.pallas_call(
        kernel,
        out_shape=tuple(
            jax.ShapeDtypeStruct(*out) for out in (*near_outs.values(), *far_outs.values())
        ),
        in_specs=[near_spec] * len(near) + [far_spec] * len(far),
        out_specs=tuple([near_spec] * len(near_outs) + [far_spec] * len(far_outs)),
        scratch_shapes=[pltpu.VMEM(*shape) for shape in scratch.values()]
        + [pltpu.SemaphoreType.DMA((40,))]
        + link_scratch,
        compiler_params=pltpu.CompilerParams(vmem_limit_bytes=VMEM_BYTES, **remote),
        cost_estimate=pl.CostEstimate(flops=flops, bytes_accessed=2**24, transcendentals=0),
        name=name,
    )(*near.values(), *far.values())
    return SimpleNamespace(**dict(zip(out_names, results)))


class Links:
    def __init__(self, sent, arrived, groups):
        self.sent, self.arrived = sent, arrived
        self.used = 0
        self.place = {axis: lax.axis_index(axis) for axis in ("dp", "seq")}
        self.sizes = groups
        barrier = pltpu.get_barrier_semaphore()
        peers = 0
        for axis, size in groups.items():
            for shift in range(1, size):
                pl.semaphore_signal(
                    barrier, inc=1, device_id=self.device(axis, shift), device_id_type=pl.DeviceIdType.MESH
                )
                peers += 1
        pl.semaphore_wait(barrier, peers)

    def peer(self, axis, shift):
        return lax.rem(self.place[axis] + shift, self.sizes[axis])

    def device(self, axis, shift):
        index = self.peer(axis, shift)
        return (index, self.place["seq"]) if axis == "dp" else (self.place["dp"], index)

    def start(self, axis, shift, origin, goal):
        copy = pltpu.make_async_remote_copy(
            src_ref=origin,
            dst_ref=goal,
            send_sem=self.sent.at[self.used],
            recv_sem=self.arrived.at[self.used],
            device_id=self.device(axis, shift),
            device_id_type=pl.DeviceIdType.MESH,
        )
        self.used += 1
        copy.start()
        return copy

    def scatter(self, axis, pick, goal):
        return [
            self.start(axis, shift, pick(self.peer(axis, shift)), goal)
            for shift in range(1, self.sizes[axis])
        ]


def split_three(value):
    high = value.astype(LOW).astype(WIDE)
    rest = value - high
    middle = rest.astype(LOW).astype(WIDE)
    return (high, middle, rest - middle)


def place_rows(parts, first, shape):
    row = lax.broadcasted_iota(jnp.int32, shape, 0)
    out = jnp.zeros(shape, WIDE)
    for offset, part in enumerate(parts):
        out = jnp.where(row == first + offset, part, out)
    return out


def document_rows(segments, tokens, is_key):
    row = lax.broadcasted_iota(jnp.int32, (16, tokens), 0)
    same = row == segments
    if is_key:
        return jnp.where(row < 4, jnp.where(same, 0.0, -BIG), 0.0)
    return jnp.where(same & (row < 4), 1.0, 0.0)


def column_peak(scores, peak):
    for start in range(0, scores.shape[0], 8):
        peak = jnp.maximum(peak, scores[start : start + 8])
    return peak


def from_column(value, low):
    if low == 0:
        return value
    return jnp.concatenate([jnp.zeros((value.shape[0], low), value.dtype), value], 1)


def attend(a, causal, prefix):
    queries, keys = a.q.shape[1], a.k.shape[1]
    width = a.context.shape[0]
    heads = width // HEAD
    tile = min(256, keys)
    tiles = keys // tile
    a.qx[:16, :queries] = document_rows(a.q_marks, queries, False).astype(LOW)
    a.kx[:, :keys] = document_rows(a.k_marks, keys, True).astype(LOW)
    start_peak = jnp.full((8, queries), -4.0 * BIG, WIDE)

    def query_of(head):
        return jnp.concatenate([a.q[rows_at(head, HEAD, a.q0), :], a.qx[:16, :queries]], 0)

    def prefix_scores(head, slot):
        if not prefix:
            return start_peak
        scores = contract(a.pair_keys[rows_at(head, HEAD), :], a.q[rows_at(head, HEAD, a.q0), :], 0, 0)
        row = lax.broadcasted_iota(jnp.int32, scores.shape, 0)
        scores = jnp.where(row < prefix, scores, -BIG)
        a.pair_scores[slot, :, :queries] = scores
        return column_peak(scores, start_peak)

    def score_tile(head, part, query, slot, peak):
        cut = slice(part * tile, (part + 1) * tile)
        low = part * tile if causal else 0
        key = jnp.concatenate([a.k[rows_at(head, HEAD, a.k0), cut], a.kx[:, cut]], 0)
        scores = contract(key, query[:, low:], 0, 0)
        if causal:
            place = lax.broadcasted_iota(jnp.int32, scores.shape, 0)
            scores = jnp.where(place <= lax.broadcasted_iota(jnp.int32, scores.shape, 1), scores, -BIG)
        a.scores[slot, cut, low:queries] = scores
        new = column_peak(scores, peak[:, low:])
        return new if low == 0 else jnp.concatenate([peak[:, :low], new], 1)

    def step(head, following, slot):
        other = 1 - slot
        query = query_of(following)
        peak = jnp.max(a.peak[slot, :, :queries], 0, keepdims=True)
        next_peak = prefix_scores(following, other)
        context = jnp.zeros((HEAD + 16, queries), WIDE)
        if prefix:
            weights = jnp.exp2(a.pair_scores[slot, :, :queries] - peak).astype(LOW)
            value = jnp.concatenate(
                [a.pair_values[rows_at(head, HEAD), :], jnp.ones((16, PAD), LOW)], 0
            )
            context = contract(value, weights, 1, 0)
        for part in range(tiles):
            next_peak = score_tile(following, part, query, other, next_peak)
            cut = slice(part * tile, (part + 1) * tile)
            low = part * tile if causal else 0
            weights = jnp.exp2(a.scores[slot, cut, low:queries] - peak[:, low:]).astype(LOW)
            value = jnp.concatenate(
                [a.v[rows_at(head, HEAD, a.v0), cut], jnp.ones((16, tile), LOW)], 0
            )
            context = context + from_column(contract(value, weights, 1, 0), low)
        a.peak[other, :, :queries] = next_peak
        total = context[HEAD : HEAD + 1]
        a.context[rows_at(head, HEAD), :] = (context[:HEAD] * (1.0 / total)).astype(LOW)
        a.lse[pl.ds(head, 1), :] = peak + jnp.log2(total)

    first = query_of(0)
    peak = prefix_scores(0, 0)
    for part in range(tiles):
        peak = score_tile(0, part, first, 0, peak)
    a.peak[0, :, :queries] = peak

    def pair(index, carry):
        step(2 * index, 2 * index + 1, 0)
        step(2 * index + 1, jnp.minimum(2 * index + 2, heads - 1), 1)
        return carry

    lax.fori_loop(0, heads // 2, pair, 0)


def block_diagonal(pairs, group, first):
    wide = GROUP * HEAD
    rows = pairs[:, first + group * wide : first + (group + 1) * wide]
    column = lax.broadcasted_iota(jnp.int32, rows.shape, 1)
    parts = [
        jnp.where((column >= member * HEAD) & (column < (member + 1) * HEAD), rows.astype(WIDE), 0.0)
        for member in range(GROUP)
    ]
    return jnp.concatenate(parts, 0).astype(LOW)


def own_columns(grads):
    column = lax.broadcasted_iota(jnp.int32, (PAD, GROUP * HEAD), 1)
    out = jnp.zeros((PAD, GROUP * HEAD), WIDE)
    for member in range(GROUP):
        own = (column >= member * HEAD) & (column < (member + 1) * HEAD)
        out = jnp.where(own, grads[member * PAD : (member + 1) * PAD], out)
    return out


def attend_back(a, causal, prefix):
    queries, keys = a.q.shape[1], a.k.shape[1]
    width = a.context.shape[0]
    heads = width // HEAD
    tile = min(256, keys // 2)
    tiles = keys // tile
    row = lax.broadcasted_iota(jnp.int32, (16, keys), 0)
    a.kx[:, :keys] = jnp.where(
        (row >= 4) & (row < 7), 1.0, document_rows(a.k_marks, keys, True)
    ).astype(LOW)
    a.vx[:, :keys] = jnp.where(row < 3, 1.0, 0.0).astype(LOW)
    documents = document_rows(a.q_marks, queries, False)

    def prepare(head, carry):
        rows = rows_at(head, HEAD)
        delta = jnp.sum(
            a.d_context[rows, :].astype(WIDE) * a.context[rows, :].astype(WIDE),
            axis=0,
            keepdims=True,
        )
        a.delta[pl.ds(head, 1), :queries] = delta
        a.dx[rows_at(head, 16), :queries] = place_rows(
            split_three(-delta), 0, (16, queries)
        ).astype(LOW)
        minus = split_three(-a.lse[pl.ds(head, 1), :])
        a.qx[rows_at(head, 16), :queries] = (
            documents + place_rows(minus, 4, (16, queries))
        ).astype(LOW)
        return carry

    lax.fori_loop(0, heads, prepare, 0)

    if prefix:
        for group in range(heads // GROUP):
            start = group * GROUP * HEAD
            own = slice(start, start + GROUP * HEAD)
            query = a.q[a.q0 + start : a.q0 + start + GROUP * HEAD, :]
            grad = a.d_context[own, :]
            pair_keys = block_diagonal(a.pairs[...], group, 0)
            pair_values = block_diagonal(a.pairs[...], group, width)
            scores = contract(pair_keys, query, 1, 0)
            gains = contract(pair_values, grad, 1, 0)
            chances, changes = [], []
            for member in range(GROUP):
                head = group * GROUP + member
                part = slice(member * PAD, (member + 1) * PAD)
                chance = jnp.exp2(scores[part] - a.lse[head : head + 1, :])
                place = lax.broadcasted_iota(jnp.int32, chance.shape, 0)
                chance = jnp.where(place < prefix, chance, 0.0)
                chances.append(chance)
                changes.append(chance * (gains[part] - a.delta[head : head + 1, :queries]))
            chances = jnp.concatenate(chances, 0).astype(LOW)
            changes = jnp.concatenate(changes, 0).astype(LOW)
            a.dq_sum[own, :queries] = contract(pair_keys, changes, 0, 0)
            a.d_pairs[:, own] = own_columns(contract(changes, query, 1, 1)) * (1.0 / LOG2E)
            a.d_pairs[:, width + start : width + start + GROUP * HEAD] = own_columns(
                contract(chances, grad, 1, 1)
            )
    else:
        a.dq_sum[:, :queries] = jnp.zeros((width, queries), WIDE)

    def front(head, part, slot):
        cut = slice(part * tile, (part + 1) * tile)
        low = part * tile if causal else 0
        query = jnp.concatenate(
            [a.q[rows_at(head, HEAD, a.q0), low:], a.qx[rows_at(head, 16), low:queries]], 0
        )
        key = jnp.concatenate([a.k[rows_at(head, HEAD, a.k0), cut], a.kx[:, cut]], 0)
        scores = contract(query, key, 0, 0)
        if causal:
            place = lax.broadcasted_iota(jnp.int32, scores.shape, 1)
            scores = jnp.where(place <= lax.broadcasted_iota(jnp.int32, scores.shape, 0), scores, -BIG)
        grad = jnp.concatenate(
            [a.d_context[rows_at(head, HEAD), low:], a.dx[rows_at(head, 16), low:queries]], 0
        )
        value = jnp.concatenate([a.v[rows_at(head, HEAD, a.v0), cut], a.vx[:, cut]], 0)
        gains = contract(grad, value, 0, 0)
        chance = jnp.exp2(scores)
        a.chances[slot, low:queries, :tile] = chance.astype(LOW)
        a.changes[slot, low:queries, :tile] = (chance * gains).astype(LOW)

    def back(head, part, slot):
        cut = slice(part * tile, (part + 1) * tile)
        low = part * tile if causal else 0
        chances = a.chances[slot, low:queries, :tile]
        changes = a.changes[slot, low:queries, :tile]
        a.dv[rows_at(head, HEAD, a.dv0), cut] = contract(
            a.d_context[rows_at(head, HEAD), low:], chances, 1, 0
        ).astype(LOW)
        a.dk[rows_at(head, HEAD, a.dk0), cut] = (
            contract(a.q[rows_at(head, HEAD, a.q0), low:], changes, 1, 0) * (1.0 / LOG2E)
        ).astype(LOW)
        a.dq_sum[rows_at(head, HEAD), low:queries] += contract(
            a.k[rows_at(head, HEAD, a.k0), cut], changes, 1, 1
        )

    def one_head(head, carry):
        for part in range(tiles):
            last = part == tiles - 1
            front(
                jnp.minimum(head + 1, heads - 1) if last else head,
                0 if last else part + 1,
                (part + 1) % 2,
            )
            back(head, part, part % 2)
        a.dq[rows_at(head, HEAD, a.dq0), :] = (
            a.dq_sum[rows_at(head, HEAD), :queries] * SCALE
        ).astype(LOW)
        return carry

    front(0, 0, 0)
    lax.fori_loop(0, heads, one_head, 0)


def project_wide(out, weight, rows, scaled, place=slice(None)):
    for cut in chunks(weight.shape[1], 256):
        result = contract(weight[:, cut], rows, 0, 1)
        if cut.start < scaled:
            result = result * (SCALE * LOG2E)
        out[cut, place] = result.astype(LOW)


def add_and_normalize(hidden, context, weight, normed, inverse):
    for cut in chunks(hidden.shape[0], CHUNK):
        summed = hidden[cut, :].astype(WIDE) + contract(context[:, cut], weight[...], 0, 0)
        result, scale = normalize(summed)
        normed[cut, :] = result.astype(LOW)
        inverse[cut, :] = scale


def feed_forward(hidden, up, down, adapter_down, adapter_up, total, slopes_of, store, narrow):
    cuts = chunks(hidden.shape[0], CHUNK)

    def block(index, first, second, factor, is_first):
        place = slopes_of(index)
        value = contract(hidden[cuts[0], :], first(), 1, 0)
        for number, cut in enumerate(cuts):
            following = None
            if number + 1 < len(cuts):
                following = contract(hidden[cuts[number + 1], :], first(), 1, 0)
            active, slope = gelu_both(value)
            place[cut, :] = slope.astype(LOW)
            if factor != 1.0:
                narrow[cut, :] = active.astype(LOW)
                active = active * factor
            product = contract(active.astype(LOW), second(), 1, 0)
            if is_first:
                total[cut, :] = hidden[cut, :].astype(WIDE) + product
            else:
                total[cut, :] += product
            value = following
        store(index)

    count = up.shape[1] // INNER
    block(0, lambda: adapter_down[...], lambda: adapter_up[...], 4.0, True)

    def main(index, carry):
        columns = rows_at(index, INNER)
        block(index + 1, lambda: up[:, columns], lambda: down[columns, :], 1.0, False)
        return carry

    lax.fori_loop(0, count, main, 0)


def finish_forward(total, normed, inverse):
    for cut in chunks(total.shape[0], CHUNK):
        result, scale = normalize(total[cut, :])
        normed[cut, :] = result.astype(LOW)
        inverse[cut, :] = scale


def feed_back(f):
    tokens = f.hidden.shape[0]
    cuts = chunks(tokens, CHUNK)
    for cut in cuts:
        value = f.grad[cut, :]
        f.low[cut, :] = value.astype(LOW)
        f.side[cut, :] = (4.0 * value).astype(LOW)

    def block(index, origin, first, second, keep):
        place = f.slopes(index)
        value = contract(origin[cuts[0], :], first(), 1, 1)
        for number, cut in enumerate(cuts):
            following = None
            if number + 1 < len(cuts):
                following = contract(origin[cuts[number + 1], :], first(), 1, 1)
            change = (value * place[cut, :].astype(WIDE)).astype(LOW)
            if keep is not None:
                keep[cut, :] = change
            f.grad[cut, :] += contract(change, second(), 1, 1)
            value = following

    block(0, f.side, lambda: f.adapter_up[...], lambda: f.adapter_down[...], f.d_narrow)
    f.d_adapter_up[...] = contract(f.narrow[...], f.side[...], 0, 0).astype(LOW)
    f.d_adapter_down[...] = contract(f.hidden[...], f.d_narrow[...], 0, 0).astype(LOW)

    def main(index, carry):
        columns = rows_at(index, INNER)
        block(index + 1, f.low, lambda: f.down[columns, :], lambda: f.up[:, columns], None)
        return carry

    lax.fori_loop(0, f.up.shape[1] // INNER, main, 0)


def normalize_back_all(grad, normed, inverse, out):
    for cut in chunks(grad.shape[0], CHUNK):
        out[cut, :] = normalize_back(
            grad[cut, :].astype(WIDE), normed[cut, :].astype(WIDE), inverse[cut, :]
        ).astype(out.dtype)


def context_back(out, weight, grad):
    value = grad[...].astype(LOW)
    for cut in chunks(weight.shape[0], 256):
        out[cut, :] = contract(weight[cut, :], value, 1, 1).astype(LOW)


def prefix_pairs(prefix, first, second, hidden, pairs, pairs_wide):
    count = prefix.shape[0]
    hidden[...] = jnp.zeros(hidden.shape, WIDE)
    hidden[:count, :] = jnp.tanh(contract(prefix[...], first[...], 1, 0))
    parts = [part.astype(LOW) for part in split_three(hidden[...])]
    pairs[...] = total_of([contract(part, second[...], 1, 0) for part in parts]).astype(LOW)
    pairs_wide[...] = total_of([contract(second[...], part, 0, 1) for part in parts]).astype(LOW)


def encoder_forward(w, group, copies):
    width = w.source.shape[2]
    share, later_share = w.source.shape[1], w.target.shape[1]
    tokens, later_tokens = share * group, later_share * group
    inner = w.enc_up.shape[1]
    narrow = w.enc_adapter_down.shape[1]
    units = w.enc_prefix_in.shape[1]
    count = w.enc_prefix.shape[0]
    blocks = 1 + inner // INNER

    def body(r):
        move = Mover(r.semaphores)
        weights = [move.start(r.enc_qkv, r.qkv_weight)]
        enc_first, dec_first = r.mid_v.at[:width, :units], r.memory_v.at[:width, :units]
        enc_second, dec_second = r.up.at[:units, : 2 * width], r.up.at[:units, 2 * width : 4 * width]
        weights.append(move.start(r.enc_prefix_in, enc_first))
        weights.append(move.start(r.enc_prefix_out, enc_second))
        weights.append(move.start(r.dec_prefix_in, dec_first))
        weights.append(move.start(r.dec_prefix_out, dec_second))
        links = Links(r.sent, r.arrived, {"seq": group})
        me = links.place["seq"]
        row = me // copies

        def tokens_of(place, size):
            return pl.ds(pl.multiple_of(place * size, size), size)

        def bring(origin, goal, size):
            own = tokens_of(me, size)
            copies_out = links.scatter("seq", lambda peer: origin.at[peer // copies], goal.at[own, :])
            return (move.start(origin.at[row], goal.at[own, :]), copies_out)

        here, sources = bring(r.source, r.x, share)
        out_weight = move.start(r.enc_out, r.out_weight)
        adapters = [
            move.start(r.enc_adapter_down, r.a_down),
            move.start(r.enc_adapter_up, r.a_up),
        ]
        pair_weight = move.start(r.cross_kv, r.pair_weight)
        for copy in weights:
            copy.wait()
        prefix_pairs(r.enc_prefix, enc_first, enc_second, r.enc_hidden, r.enc_pairs, r.enc_pairs_wide)
        prefix_pairs(r.dec_prefix, dec_first, dec_second, r.dec_hidden, r.dec_pairs, r.dec_pairs_wide)
        ups = [move.start(r.enc_up, r.up), move.start(r.enc_down, r.down)]
        here.wait()
        if share % 128 == 0:
            place = tokens_of(me, share)
            project_wide(r.qkv_v, r.qkv_weight, r.x[place, :], width, place)
            for shift, copy in enumerate(sources, 1):
                copy.wait()
                place = tokens_of(lax.rem(me + group - shift, group), share)
                project_wide(r.qkv_v, r.qkv_weight, r.x[place, :], width, place)
        else:
            for copy in sources:
                copy.wait()
            project_wide(r.qkv_v, r.qkv_weight, r.x[...], width)
        later = [
            bring(r.target, r.target_rows, later_share),
            bring(r.cotangent, r.cotangent_rows, later_share),
        ]
        outs = [move.start(r.qkv_v, r.qkv)]
        marks = r.marks[pl.ds(row, 1), :]
        attend(
            SimpleNamespace(
                q=r.qkv_v, k=r.qkv_v, v=r.qkv_v, q0=0, k0=width, v0=2 * width,
                q_marks=marks, k_marks=marks, pair_keys=r.enc_pairs_wide.at[:width],
                pair_values=r.enc_pairs_wide.at[width:],
                context=r.context_v, lse=r.lse, qx=r.qx, kx=r.kx, scores=r.scores,
                pair_scores=r.pair_scores, peak=r.peak,
            ),
            False,
            count,
        )
        outs.append(move.start(r.context_v, r.context))
        out_weight.wait()
        add_and_normalize(r.x, r.context_v, r.out_weight, r.mid_v, r.mid_inverse)
        outs.append(move.start(r.mid_v, r.mid))
        for copy in adapters + ups:
            copy.wait()
        feed_forward(
            r.mid_v, r.up, r.down, r.a_down, r.a_up, r.total,
            lambda index: r.slopes_v.at[index], lambda index: None, r.narrow_v,
        )
        outs.append(move.start(r.slopes_v, r.slopes))
        outs.append(move.start(r.narrow_v, r.narrow))
        finish_forward(r.total, r.memory_v, r.memory_inverse)
        outs.append(move.start(r.memory_v, r.memory))
        pair_weight.wait()
        project_wide(r.pairs_v, r.pair_weight, r.memory_v[...], 0)
        outs.append(move.start(r.pairs_v, r.memory_pairs))
        for own, remote in later:
            own.wait()
            for copy in remote:
                copy.wait()
        for copy in outs:
            copy.wait()

    return run_kernel(
        body,
        "encoder_forward",
        near=dict(marks=w.source_segments, enc_prefix=w.enc_prefix, dec_prefix=w.dec_prefix),
        far=dict(
            source=w.source, target=w.target, cotangent=w.cotangent, enc_qkv=w.enc_qkv,
            enc_out=w.enc_out, enc_up=w.enc_up, enc_down=w.enc_down,
            enc_adapter_down=w.enc_adapter_down, enc_adapter_up=w.enc_adapter_up,
            cross_kv=w.cross_kv, enc_prefix_in=w.enc_prefix_in, enc_prefix_out=w.enc_prefix_out,
            dec_prefix_in=w.dec_prefix_in, dec_prefix_out=w.dec_prefix_out,
        ),
        near_outs=dict(
            lse=((16, tokens), WIDE), mid_inverse=((tokens, 1), WIDE),
            memory_inverse=((tokens, 1), WIDE),
            enc_hidden=((PAD, units), WIDE), enc_pairs=((PAD, 2 * width), LOW),
            dec_hidden=((PAD, units), WIDE), dec_pairs=((PAD, 2 * width), LOW),
            dec_pairs_wide=((2 * width, PAD), LOW),
        ),
        far_outs=dict(
            qkv=((3 * width, tokens), LOW), context=((width, tokens), LOW), mid=((tokens, width), LOW),
            slopes=((blocks, tokens, INNER), LOW), narrow=((tokens, narrow), LOW),
            memory=((tokens, width), LOW), memory_pairs=((2 * width, tokens), LOW),
            target_rows=((later_tokens, width), LOW), cotangent_rows=((later_tokens, width), LOW),
        ),
        scratch=dict(
            x=((tokens, width), LOW), qkv_weight=((width, 3 * width), LOW),
            enc_pairs_wide=((2 * width, PAD), LOW),
            out_weight=((width, width), LOW), a_down=((width, narrow), LOW),
            a_up=((narrow, width), LOW), up=((width, inner), LOW), down=((inner, width), LOW),
            pair_weight=((width, 2 * width), LOW), qkv_v=((3 * width, tokens), LOW),
            context_v=((width, tokens), LOW), mid_v=((tokens, width), LOW),
            slopes_v=((blocks, tokens, INNER), LOW), narrow_v=((tokens, narrow), LOW),
            memory_v=((tokens, width), LOW), pairs_v=((2 * width, tokens), LOW),
            total=((tokens, width), WIDE), qx=((16, tokens), LOW), kx=((16, tokens), LOW),
            scores=((2, tokens, tokens), WIDE), pair_scores=((2, PAD, tokens), WIDE),
            peak=((2, 8, tokens), WIDE),
        ),
        flops=2 * tokens * width * 11776 + 4 * tokens * tokens * width,
        links=3 * (group - 1),
        collective=0,
    )


def decoder(forward, w, copies):
    tokens, width = forward.target_rows.shape
    keys = forward.memory_pairs.shape[1]
    count = w.dec_prefix.shape[0]
    inner = w.dec_up.shape[1]
    narrow = w.dec_adapter_down.shape[1]
    blocks = 1 + inner // INNER
    heads = width // HEAD

    def body(r):
        move = Mover(r.semaphores)
        ins = [move.start(r.target, r.x), move.start(r.dec_qkv, r.qkv_weight)]
        for copy in ins:
            copy.wait()
        out_weight = move.start(r.dec_out, r.out_weight)
        crosses = [
            move.start(r.cross_q, r.query_weight),
            move.start(r.memory_pairs, r.pairs_v),
            move.start(r.cross_out, r.cross_out_weight),
        ]
        adapters = [
            move.start(r.dec_adapter_down, r.a_down),
            move.start(r.dec_adapter_up, r.a_up),
        ]
        ups = [move.start(r.dec_up, r.up), move.start(r.dec_down, r.down)]
        cotangents = move.start(r.cotangent, r.cotangent_v)
        project_wide(r.qkv, r.qkv_weight, r.x[...], width)
        row = pl.ds(lax.axis_index("seq") // copies, 1)
        marks, source_marks = r.marks[row, :], r.source_marks[row, :]
        shared = dict(
            qx=r.qx, kx=r.kx, scores=r.scores, pair_scores=r.pair_scores, peak=r.peak, dx=r.dx,
            vx=r.vx, delta=r.delta, dq_sum=r.dq_sum, chances=r.chances, changes=r.changes,
            d_context=r.d_context,
        )
        self_part = SimpleNamespace(
            q=r.qkv, k=r.qkv, v=r.qkv, q0=0, k0=width, v0=2 * width,
            q_marks=marks, k_marks=marks, pair_keys=r.pairs_wide.at[:width],
            pair_values=r.pairs_wide.at[width:], pairs=r.pairs, context=r.context, lse=r.lse,
            dq=r.d_qkv, dk=r.d_qkv, dv=r.d_qkv, dq0=0, dk0=width, dv0=2 * width,
            d_pairs=r.d_pairs, **shared,
        )
        attend(self_part, True, count)
        out_weight.wait()
        add_and_normalize(r.x, r.context, r.out_weight, r.mid, r.mid_inverse)
        for copy in crosses:
            copy.wait()
        project_wide(r.query, r.query_weight, r.mid[...], width)
        cross_part = SimpleNamespace(
            q=r.query, k=r.pairs_v, v=r.pairs_v, q0=0, k0=0, v0=width,
            q_marks=marks, k_marks=source_marks, context=r.cross_context, lse=r.cross_lse,
            dq=r.d_query, dk=r.d_pairs_v, dv=r.d_pairs_v, dq0=0, dk0=0, dv0=width, **shared,
        )
        attend(cross_part, False, 0)
        add_and_normalize(r.mid, r.cross_context, r.cross_out_weight, r.crossed, r.crossed_inverse)
        for copy in adapters + ups + [cotangents]:
            copy.wait()
        feed_forward(
            r.crossed, r.up, r.down, r.a_down, r.a_up, r.total,
            lambda index: r.slopes.at[index], lambda index: None, r.narrow,
        )
        finish_forward(r.total, r.out_v, r.out_inverse)
        outs = [move.start(r.out_v, r.out)]
        normalize_back_all(r.cotangent_v, r.out_v, r.out_inverse, r.total)
        feed_back(
            SimpleNamespace(
                grad=r.total, low=r.low, side=r.side, hidden=r.crossed, narrow=r.narrow, up=r.up,
                down=r.down, adapter_down=r.a_down, adapter_up=r.a_up,
                slopes=lambda index: r.slopes.at[index], d_adapter_down=r.d_a_down,
                d_adapter_up=r.d_a_up, d_narrow=r.d_narrow,
            )
        )
        outs.append(move.start(r.d_a_down, r.adapter_down_grad))
        outs.append(move.start(r.d_a_up, r.adapter_up_grad))
        normalize_back_all(r.total, r.crossed, r.crossed_inverse, r.total)
        context_back(r.d_context, r.cross_out_weight, r.total)
        attend_back(cross_part, False, 0)
        outs.append(move.start(r.d_pairs_v, r.memory_pairs_grad))
        for cut in chunks(tokens, CHUNK):
            r.total[cut, :] += contract(r.d_query[:, cut], r.query_weight[...], 0, 1)
        normalize_back_all(r.total, r.mid, r.mid_inverse, r.total)
        context_back(r.d_context, r.out_weight, r.total)
        attend_back(self_part, True, count)
        for cut in chunks(tokens, CHUNK):
            r.x[cut, :] = (
                r.total[cut, :] + contract(r.d_qkv[:, cut], r.qkv_weight[...], 0, 1)
            ).astype(LOW)
        outs.append(move.start(r.x, r.target_grad))
        for copy in outs:
            copy.wait()

    return run_kernel(
        body,
        "decoder",
        near=dict(
            marks=w.target_segments, source_marks=w.source_segments,
            pairs_wide=forward.dec_pairs_wide, pairs=forward.dec_pairs,
        ),
        far=dict(
            target=forward.target_rows, cotangent=forward.cotangent_rows,
            memory_pairs=forward.memory_pairs, dec_qkv=w.dec_qkv,
            dec_out=w.dec_out, cross_q=w.cross_q, cross_out=w.cross_out, dec_up=w.dec_up,
            dec_down=w.dec_down, dec_adapter_down=w.dec_adapter_down,
            dec_adapter_up=w.dec_adapter_up,
        ),
        near_outs=dict(d_pairs=((PAD, 2 * width), WIDE)),
        far_outs=dict(
            out=((tokens, width), LOW), target_grad=((tokens, width), LOW),
            memory_pairs_grad=((2 * width, keys), LOW), adapter_down_grad=((width, narrow), LOW),
            adapter_up_grad=((narrow, width), LOW),
        ),
        scratch=dict(
            x=((tokens, width), LOW), cotangent_v=((tokens, width), LOW),
            qkv_weight=((width, 3 * width), LOW), out_weight=((width, width), LOW),
            query_weight=((width, width), LOW), cross_out_weight=((width, width), LOW),
            pairs_v=((2 * width, keys), LOW), a_down=((width, narrow), LOW),
            a_up=((narrow, width), LOW), up=((width, inner), LOW), down=((inner, width), LOW),
            qkv=((3 * width, tokens), LOW), context=((width, tokens), LOW),
            mid=((tokens, width), LOW), mid_inverse=((tokens, 1), WIDE),
            query=((width, tokens), LOW), cross_context=((width, tokens), LOW),
            crossed=((tokens, width), LOW), crossed_inverse=((tokens, 1), WIDE),
            out_v=((tokens, width), LOW), out_inverse=((tokens, 1), WIDE),
            slopes=((blocks, tokens, INNER), LOW), narrow=((tokens, narrow), LOW),
            low=((tokens, width), LOW), side=((tokens, width), LOW), d_narrow=((tokens, narrow), LOW),
            d_a_down=((width, narrow), LOW), d_a_up=((narrow, width), LOW),
            total=((tokens, width), WIDE), lse=((16, tokens), WIDE), cross_lse=((16, tokens), WIDE),
            d_context=((width, tokens), LOW), d_query=((width, tokens), LOW),
            d_pairs_v=((2 * width, keys), LOW), d_qkv=((3 * width, tokens), LOW),
            qx=((heads * 16, tokens), LOW), kx=((16, keys), LOW),
            scores=((2, keys, tokens), WIDE), pair_scores=((2, PAD, tokens), WIDE),
            peak=((2, 8, tokens), WIDE), dx=((heads * 16, tokens), LOW), vx=((16, keys), LOW),
            delta=((16, tokens), WIDE), dq_sum=((width, tokens), WIDE),
            chances=((2, tokens, 256), LOW), changes=((2, tokens, 256), LOW),
        ),
        flops=4 * tokens * width * 11776 + 14 * tokens * (keys + tokens) * width,
    )


def encoder_feed_back(dec, forward, w, group):
    tokens, width = forward.memory.shape
    inner = w.enc_up.shape[1]
    narrow = w.enc_adapter_down.shape[1]
    blocks = 1 + inner // INNER

    def body(r):
        move = Mover(r.semaphores)
        firsts = [
            move.start(r.memory_pairs_grad, r.d_pairs),
            move.start(r.cross_kv, r.pair_weight),
            move.start(r.memory, r.memory_v),
        ]
        adapters = [
            move.start(r.enc_adapter_down, r.a_down),
            move.start(r.enc_adapter_up, r.a_up),
            move.start(r.narrow, r.narrow_v),
            move.start(r.mid, r.mid_v),
        ]
        ups = [
            move.start(r.slopes, r.slopes_v),
            move.start(r.enc_down, r.down),
            move.start(r.enc_up, r.up),
            move.start(r.enc_out, r.out_weight),
        ]
        links = Links(r.sent, r.arrived, {"seq": group})
        me = links.place["seq"]
        crossing = []
        for origin, goal in ((r.out, r.out_all), (r.target_grad, r.target_grad_all)):
            crossing += links.scatter("seq", lambda peer: origin.at[peer], goal.at[me])
            crossing.append(move.start(origin.at[me], goal.at[me]))
        for copy in firsts:
            copy.wait()
        for cut in chunks(tokens, CHUNK):
            grad = contract(r.d_pairs[:, cut], r.pair_weight[...], 0, 1)
            r.total[cut, :] = normalize_back(
                grad, r.memory_v[cut, :].astype(WIDE), r.memory_inverse[cut, :]
            )
        for copy in adapters + ups:
            copy.wait()
        feed_back(
            SimpleNamespace(
                grad=r.total, low=r.low, side=r.side, hidden=r.mid_v, narrow=r.narrow_v, up=r.up,
                down=r.down, adapter_down=r.a_down, adapter_up=r.a_up,
                slopes=lambda index: r.slopes_v.at[index], d_adapter_down=r.d_a_down,
                d_adapter_up=r.d_a_up, d_narrow=r.d_narrow,
            )
        )
        outs = [
            move.start(r.d_a_down, r.adapter_down_grad),
            move.start(r.d_a_up, r.adapter_up_grad),
        ]
        normalize_back_all(r.total, r.mid_v, r.mid_inverse, r.low)
        outs.append(move.start(r.low, r.summed_grad))
        context_back(r.d_context_v, r.out_weight, r.low)
        outs.append(move.start(r.d_context_v, r.d_context))
        for copy in outs + crossing:
            copy.wait()

    return run_kernel(
        body,
        "encoder_feed_back",
        near=dict(mid_inverse=forward.mid_inverse, memory_inverse=forward.memory_inverse),
        far=dict(
            out=dec.out.reshape(group, -1, width), target_grad=dec.target_grad.reshape(group, -1, width),
            memory_pairs_grad=dec.memory_pairs_grad, memory=forward.memory, mid=forward.mid,
            slopes=forward.slopes, narrow=forward.narrow, cross_kv=w.cross_kv,
            enc_out=w.enc_out, enc_up=w.enc_up, enc_down=w.enc_down,
            enc_adapter_down=w.enc_adapter_down, enc_adapter_up=w.enc_adapter_up,
        ),
        near_outs={},
        far_outs=dict(
            summed_grad=((tokens, width), LOW), d_context=((width, tokens), LOW),
            adapter_down_grad=((width, narrow), LOW), adapter_up_grad=((narrow, width), LOW),
            out_all=((group, dec.out.shape[0] // group, width), LOW),
            target_grad_all=((group, dec.out.shape[0] // group, width), LOW),
        ),
        scratch=dict(
            d_pairs=((2 * width, tokens), LOW), pair_weight=((width, 2 * width), LOW),
            memory_v=((tokens, width), LOW), mid_v=((tokens, width), LOW),
            slopes_v=((blocks, tokens, INNER), LOW), narrow_v=((tokens, narrow), LOW),
            out_weight=((width, width), LOW), a_down=((width, narrow), LOW),
            a_up=((narrow, width), LOW), up=((width, inner), LOW), down=((inner, width), LOW),
            low=((tokens, width), LOW), side=((tokens, width), LOW), d_narrow=((tokens, narrow), LOW),
            d_a_down=((width, narrow), LOW), d_a_up=((narrow, width), LOW),
            total=((tokens, width), WIDE), d_context_v=((width, tokens), LOW),
        ),
        flops=2 * tokens * width * 9728,
        links=2 * (group - 1),
        collective=1,
    )


def encoder_attend_back(feed, forward, w, group, copies):
    tokens, width = feed.summed_grad.shape
    share = tokens // group
    count = w.enc_prefix.shape[0]
    heads = width // HEAD

    def body(r):
        move = Mover(r.semaphores)
        firsts = [
            move.start(r.qkv, r.qkv_v),
            move.start(r.d_context, r.d_context_v),
            move.start(r.context, r.context_v),
        ]
        lasts = [move.start(r.enc_qkv, r.qkv_weight), move.start(r.summed_grad, r.summed_v)]
        links = Links(r.sent, r.arrived, {"seq": group})
        me = links.place["seq"]
        marks = r.marks[pl.ds(me // copies, 1), :]
        for copy in firsts:
            copy.wait()
        attend_back(
            SimpleNamespace(
                q=r.qkv_v, k=r.qkv_v, v=r.qkv_v, q0=0, k0=width, v0=2 * width,
                q_marks=marks, k_marks=marks, pairs=r.pairs, context=r.context_v, lse=r.lse,
                d_context=r.d_context_v, dq=r.d_qkv, dk=r.d_qkv, dv=r.d_qkv, dq0=0, dk0=width,
                dv0=2 * width, d_pairs=r.d_pairs, qx=r.qx, kx=r.kx, dx=r.dx, vx=r.vx,
                delta=r.delta, dq_sum=r.dq_sum, chances=r.chances, changes=r.changes,
            ),
            False,
            count,
        )
        for copy in lasts:
            copy.wait()
        for cut in chunks(tokens, CHUNK):
            r.summed_v[cut, :] = (
                r.summed_v[cut, :].astype(WIDE)
                + contract(r.d_qkv[:, cut], r.qkv_weight[...], 0, 1)
            ).astype(LOW)

        def tokens_of(place):
            return r.summed_v.at[pl.ds(pl.multiple_of(place * share, share), share), :]

        crossing = links.scatter("seq", tokens_of, r.source_grad.at[me])
        crossing.append(move.start(tokens_of(me), r.source_grad.at[me]))
        for copy in crossing:
            copy.wait()

    return run_kernel(
        body,
        "encoder_attend_back",
        near=dict(marks=w.source_segments, pairs=forward.enc_pairs, lse=forward.lse),
        far=dict(
            qkv=forward.qkv, d_context=feed.d_context, context=forward.context,
            enc_qkv=w.enc_qkv, summed_grad=feed.summed_grad,
        ),
        near_outs=dict(d_pairs=((PAD, 2 * width), WIDE)),
        far_outs=dict(source_grad=((group, share, width), LOW)),
        scratch=dict(
            qkv_v=((3 * width, tokens), LOW), d_context_v=((width, tokens), LOW),
            context_v=((width, tokens), LOW), qkv_weight=((width, 3 * width), LOW),
            summed_v=((tokens, width), LOW), d_qkv=((3 * width, tokens), LOW),
            qx=((heads * 16, tokens), LOW), kx=((16, tokens), LOW),
            dx=((heads * 16, tokens), LOW), vx=((16, tokens), LOW), delta=((16, tokens), WIDE),
            dq_sum=((width, tokens), WIDE), chances=((2, tokens, 256), LOW),
            changes=((2, tokens, 256), LOW),
        ),
        flops=2 * tokens * width * 2304 + 20 * tokens * tokens * width,
        links=group - 1,
        collective=2,
    )


def prefix_backward(prefix, prefix_in, prefix_out, hidden, pair_grad, place, count):
    def share(value, axis):
        size = value.shape[axis] // count
        return lax.dynamic_slice_in_dim(value, place * size, size, axis).astype(WIDE)

    exact = functools.partial(jnp.matmul, precision=lax.Precision.HIGHEST)
    out_grad = exact(share(hidden, 1).T, pair_grad)
    hidden_grad = exact(pair_grad, prefix_out.astype(WIDE).T) * (1.0 - hidden * hidden)
    in_grad = exact(share(prefix, 1).T, hidden_grad)
    embed_grad = exact(hidden_grad, share(prefix_in, 0).T)
    return (embed_grad, in_grad, out_grad)


def total_of(values):
    return functools.reduce(lambda left, right: left + right, values)


NAMES = (
    "source",
    "target",
    "source_segments",
    "target_segments",
    "cotangent",
    "enc_qkv",
    "enc_out",
    "enc_up",
    "enc_down",
    "dec_qkv",
    "dec_out",
    "cross_q",
    "cross_kv",
    "cross_out",
    "dec_up",
    "dec_down",
    "enc_prefix",
    "enc_prefix_in",
    "enc_prefix_out",
    "enc_adapter_down",
    "enc_adapter_up",
    "dec_prefix",
    "dec_prefix_in",
    "dec_prefix_out",
    "dec_adapter_down",
    "dec_adapter_up",
)


def shards(*operands, count):
    w = SimpleNamespace(**dict(zip(NAMES, operands)))
    place = lax.axis_index("seq")
    copies = count // w.source.shape[0]
    forward = encoder_forward(w, count, copies)
    dec = decoder(forward, w, copies)
    feed = encoder_feed_back(dec, forward, w, count)
    attended = encoder_attend_back(feed, forward, w, count, copies)
    share = 1.0 / copies

    def gathered(grad):
        grad = (grad.astype(WIDE) * share).astype(LOW)
        return lax.psum(lax.psum_scatter(grad, "seq", scatter_dimension=0, tiled=True), "dp").astype(WIDE)

    adapters = [
        gathered(grad)
        for grad in (
            feed.adapter_down_grad, feed.adapter_up_grad, dec.adapter_down_grad, dec.adapter_up_grad
        )
    ]
    used = w.enc_prefix.shape[0]
    enc_pair_grad, dec_pair_grad = lax.psum(
        (attended.d_pairs[:used] * share, dec.d_pairs[:used] * share), ("dp", "seq")
    )
    enc_prefix_grads = prefix_backward(
        w.enc_prefix, w.enc_prefix_in, w.enc_prefix_out, forward.enc_hidden[:used], enc_pair_grad, place, count
    )
    dec_prefix_grads = prefix_backward(
        w.dec_prefix, w.dec_prefix_in, w.dec_prefix_out, forward.dec_hidden[:used], dec_pair_grad, place, count
    )
    return (
        feed.out_all[::copies],
        attended.source_grad[::copies].astype(WIDE),
        feed.target_grad_all[::copies].astype(WIDE),
        *enc_prefix_grads,
        adapters[0],
        adapters[1],
        *dec_prefix_grads,
        adapters[2],
        adapters[3],
    )


def solution(mesh):
    rows = P("dp", "seq", None)
    marks = P("dp", None)
    in_specs = (rows, rows, marks, marks, rows) + (P(),) * 21
    across, down = P(None, "seq"), P("seq", None)
    layer = (across, down, down, down, down)
    return jax.shard_map(
        functools.partial(shards, count=mesh.shape["seq"]),
        mesh=mesh,
        in_specs=in_specs,
        out_specs=(rows, rows, rows) + layer + layer,
        check_vma=False,
    )
```

time: 725 us -> 603 us (0.83)
  matrix products: 186 us -> 13.6 us
  Pallas kernels: 112 us -> 262 us
  local copies, waits for them, and re-layouts: 113 us -> 0.91 us
  waiting for transfers between devices: 204 us -> 291 us
  other arithmetic: 54 us -> 9.56 us
  starting transfers between devices: 31.2 us -> 0.54 us
    dot_general x36 -> x0, matrix products: 171 us -> none  [the longest x6 51.9 us: back_through(): jnp.einsum('ln,dn->ld', gradient, weight, preferred_element_type=WIDE)]
    pallas_call x6 -> x4, Pallas kernels: 112 us -> 262 us  [run_kernel(): pl.pallas_call(kernel, out_shape=tuple((jax.ShapeDtypeStruct(*out) for ou...]
    psum x2, waiting for transfers between devices: 62.3 us -> 168 us  [the longest x1 135 us: shards(): lax.psum((attended.d_pairs[:used] * share, dec.d_pairs[:used] * share), (...]
    unnamed x142 -> x19, local copies, waits for them, and re-layouts: 46.8 us -> 0.91 us
    all_to_all x6 -> x0, starting transfers between devices: 30.4 us -> none  [the longest x3 16.1 us: bring(): lax.all_to_all(jnp.repeat(value, copies, axis=0), 'seq', 0, 1, tiled=True)]
    unnamed x6 -> x0, other arithmetic: 27 us -> none
    reshape x12 -> x0, local copies, waits for them, and re-layouts: 23.5 us -> none  [the longest x4 8.84 us: from_block_diagonal(): spread = grads.reshape(heads // GROUP, GROUP, PAD, GROUP, HEAD)]
    all_to_all x6 -> x0, waiting for transfers between devices: 16.8 us -> none  [the longest x3 13.1 us: bring(): lax.all_to_all(jnp.repeat(value, copies, axis=0), 'seq', 0, 1, tiled=True)]
  transfers between devices with their start and end apart: 12 -> 6, of which waited for: 8 -> 4; matrix products, arithmetic and copies ran while one was open for 24% -> 3% of each run, Pallas kernels for 1% -> 0%
where the time goes in v2:
time: 603 us; the launch traced here: 594 us
  waiting for transfers between devices  291 us (48%)
  Pallas kernels  262 us (43%)
  between operations  16.3 us (3%)
  matrix products  13.6 us (2%)
  other arithmetic  9.56 us (2%)
    pallas_call x4, Pallas kernels, run_kernel(): pl.pallas_call(kernel, out_shape=tuple((jax.ShapeDtypeStruct(*out) for ou...  262 us
    psum x1, waiting for transfers between devices, shards(): lax.psum((attended.d_pairs[:used] * share, dec.d_pairs[:used] * share), (...  135 us
    reduce_scatter x4, waiting for transfers between devices, gathered(): lax.psum_scatter(grad, 'seq', scatter_dimension=0, tiled=True)  121 us
    psum x1, waiting for transfers between devices, gathered(): lax.psum(lax.psum_scatter(grad, 'seq', scatter_dimension=0, tiled=True),...  32.8 us
  transfers between devices with their start and end apart: 6, of which 4 were waited for; matrix products, arithmetic and copies ran while one was open for 3% of the time, Pallas kernels for 0%

profile of v2, /device:TPU:0, one launch (start us, length us, event | category | flops | bytes accessed | tf_op | source)
XLA Modules:
  0.0 594.0 jit_solution(10260112115238401999)
XLA Ops:
  8.1 75.3 %encoder_forward.1 = (f32[16,1024]{1,0:T(8,128)}, f32[1024,1]{1,0:T(8,128)}, f32[1024,1]{1,0:T(8,128)}, f32[32,512]{1,0:T(8,128)}, bf16[32,1536]{1,0:T(8,128)(2,...) custom-call(s32[8,1024]{1,0:T(8,128)} %refs_0_.5, ...), custom_call_target="tpu_custom_call" | custom-call | flops 21743271936 | bytes 16777216 | tf_op jit(solution)/shard_map/encoder_forward/pallas_call | solution.py:91
  83.4 70.9 %decoder.1 = (f32[32,1536]{1,0:T(8,128)}, bf16[512,768]{1,0:T(8,128)(2,1)}, bf16[512,768]{1,0:T(8,128)(2,1)}, bf16[1536,1024]{1,0:T(8,128)(2,1)}, bf16[768,512]{1,0:T(8,128)(2,1)}, /*index=5*/bf16[512,768]{1,0:T(8,128)(2,1)}) custom-call(s32[8,512]{1,0:T(8,128)} %refs_0_.4, s32[8,1024]{1,0:T(8,128)} %refs_0_.5, bf16[1536,32]{1,0:T(8,128)(2,1)} %get-tuple-element.46.refs_2_, ...), custom_call_target="tpu_custom_call" | custom-call | flops 26977763328 | bytes 16777216 | tf_op jit(solution)/shard_map/decoder/pallas_call | solution.py:91
  154.3 42.7 %encoder_feed_back.1 = (bf16[1024,768]{1,0:T(8,128)(2,1)}, bf16[768,1024]{1,0:T(8,128)(2,1)}, bf16[768,512]{1,0:T(8,128)(2,1)}, bf16[512,768]{1,0:T(8,128)(2,1)}...) custom-call(f32[1024,1]{1,0:T(8,128)} %get-tuple-element.44.refs_0_, f32[1024,1]{1,0:T(8,128)} %get-tuple-element.45.refs_1_, ...), custom_call_target="tpu_custom_call" | custom-call | flops 15300820992 | bytes 16777216 | tf_op jit(solution)/shard_map/encoder_feed_back/pallas_call | solution.py:91
  197.0 73.5 %encoder_attend_back.1 = (f32[32,1536]{1,0:T(8,128)}, bf16[8,128,768]{2,1,0:T(8,128)(2,1)}) custom-call(s32[8,1024]{1,0:T(8,128)} %refs_0_.5, bf16[32,1536]{1,0:T(8,128)(2,1)} %get-tuple-element.59.refs_1_, f32[16,1024]{1,0:T(8,128)} %get-tuple-element.60.refs_2_, bf16[2304,1024]{1,0:T(8,128)(2,1)} %get-tuple-element.61.refs_3_, ...), custom_call_target="tpu_custom_call" | custom-call | flops 19730006016 | bytes 16777216 | tf_op jit(solution)/shard_map/encoder_attend_back/pallas_call | solution.py:91
  272.3 0.7 reduce-scatter.9.cloned.1.call-update
  273.4 1.9 convert_element_type.12
  275.4 1.3 convert_element_type.13
  276.6 134.9 %all-reduce.5.cloned.1.call-done = (f32[30,1536]{1,0:T(8,128)}, f32[30,1536]{1,0:T(8,128)}) async-done(((f32[30,1536]{1,0:T(8,128)}, f32[30,1536]{1,0:T(8,128)}), (f32[30,1536]{1,0:T(8,128)}, f32[30,1536]{1,0:T(8,128)})) %all-reduce.5.cloned.1.call-update) | async-done | bytes 368656 | tf_op jit(solution)/shard_map/psum | solution.py:1014
  411.5 2.4 convolution_multiply_fusion
  414.0 1.8 fusion
  415.7 1.7 fusion.8
  417.5 1.5 convolution_multiply_fusion.1
  418.9 1.8 fusion.10
  420.8 1.3 fusion.4
  422.1 1.3 fusion.6
  423.4 55.8 %reduce-scatter.11.cloned.1.call-done = bf16[64,768]{1,0:T(8,128)(2,1)} async-done(((bf16[512,768]{1,0:T(8,128)(2,1)}), bf16[64,768]{1,0:T(8,128)(2,1)}) %reduce-scatter.11.cloned.1.call-update) | async-done | bytes 98320 | tf_op jit(solution)/shard_map/reduce_scatter | solution.py:1005
  479.2 64.9 %reduce-scatter.9.cloned.1.call-done = bf16[96,512]{1,0:T(8,128)(2,1)} async-done(((bf16[768,512]{1,0:T(8,128)(2,1)}), bf16[96,512]{1,0:T(8,128)(2,1)}) %reduce-scatter.9.cloned.1.call-update) | async-done | bytes 98320 | tf_op jit(solution)/shard_map/reduce_scatter | solution.py:1005
  544.1 1.7 fusion.2
  545.9 32.8 %all-reduce.7.cloned.1.call-done = (bf16[96,512]{1,0:T(8,128)(2,1)}, bf16[64,768]{1,0:T(8,128)(2,1)}, bf16[96,512]{1,0:T(8,128)(2,1)}, bf16[64,768]{1,0:T(8,128)(2,1)}) async-done(((bf16[96,512]{1,0:T(8,128)(2,1)}, bf16[64,768]{1,0:T(8,128)(2,1)}, bf16[96,512]{1,0:T(8,128)(2,1)}, bf16[64,768]{1,0:T(8,128)(2,1)}), (bf16[96,512]{1,0:T(8,128)(2,1)}, bf16[64,768]{1,0:T(8,128)(2,1)}, bf16[96,512]{1,0:T(8,128)(2,1)}, ...) | async-done | bytes 393232 | tf_op jit(solution)/shard_map/psum | solution.py:1005
  578.7 1.6 convert_element_type.14
  580.3 1.6 convert_element_type.15
  581.9 1.6 convert_element_type.16
  583.5 1.6 convert_element_type.17
  585.0 0.9 copy.46
  (31 shorter events, 2.2 us)
Async XLA Ops:
  8.0 403.5 %all-reduce.5.cloned.1.call-start = ((), (), s32[]{:S(2)}) async-start(), calls=%async_computation.8 | async-start | bytes 786432 | tf_op jit(solution)/shard_map/psum | solution.py:1014
  270.6 152.9 %reduce-scatter.5.cloned.1.call-start = ((), (), s32[]{:S(2)}) async-start(), calls=%async_computation.4 | async-start | bytes 884736 | tf_op jit(solution)/shard_map/reduce_scatter | solution.py:1005
  270.6 2.8 copy-start.2
  271.1 152.3 %reduce-scatter.7.cloned.1.call-start = ((), (), s32[]{:S(2)}) async-start(), calls=%async_computation.5 | async-start | bytes 884736 | tf_op jit(solution)/shard_map/reduce_scatter | solution.py:1005
  271.7 207.5 %reduce-scatter.11.cloned.1.call-start = ((), (), s32[]{:S(2)}) async-start(), calls=%async_computation.7 | async-start | bytes 884736 | tf_op jit(solution)/shard_map/reduce_scatter | solution.py:1005
  272.3 271.8 %reduce-scatter.9.cloned.1.call-start = ((), (), s32[]{:S(2)}) async-start(), calls=%async_computation.6 | async-start | bytes 884736 | tf_op jit(solution)/shard_map/reduce_scatter | solution.py:1005
  273.0 305.7 %all-reduce.7.cloned.1.call-start = ((), (), s32[]{:S(2)}) async-start(), calls=%async_computation.9 | async-start | bytes 786432 | tf_op jit(solution)/shard_map/psum | solution.py:1005
  273.4 2.0 copy-start.6
  275.4 136.2 %copy-start = (bf16[512,1536]{1,0:T(8,128)(2,1)S(1)}, bf16[512,1536]{1,0:T(8,128)(2,1)}, u32[]{:S(2)}) copy-start(bf16[512,1536]{1,0:T(8,128)(2,1)} %refs_16_.1) | copy-start | bytes 4718596
  275.4 136.2 %copy-start.8 = (f32[32,512]{1,0:T(8,128)S(1)}, f32[32,512]{1,0:T(8,128)}, u32[]{:S(2)}) copy-start(f32[32,512]{1,0:T(8,128)} %get-tuple-element.72) | copy-start | bytes 196612
  276.6 140.8 %copy-start.1 = (bf16[512,1536]{1,0:T(8,128)(2,1)S(1)}, bf16[512,1536]{1,0:T(8,128)(2,1)}, u32[]{:S(2)}) copy-start(bf16[512,1536]{1,0:T(8,128)(2,1)} %refs_14_.3) | copy-start | bytes 4718596
  276.6 140.8 %copy-start.7 = (f32[32,512]{1,0:T(8,128)S(1)}, f32[32,512]{1,0:T(8,128)}, u32[]{:S(2)}) copy-start(f32[32,512]{1,0:T(8,128)} %get-tuple-element.68) | copy-start | bytes 196612
  411.5 5.9 %copy-start.4 = (f32[30,1536]{1,0:T(8,128)S(1)}, f32[30,1536]{1,0:T(8,128)}, u32[]{:S(2)}) copy-start(f32[30,1536]{1,0:T(8,128)} %get-tuple-element.75) | copy-start | bytes 552964
  413.9 6.8 %copy-start.5 = (f32[30,1536]{1,0:T(8,128)S(1)}, f32[30,1536]{1,0:T(8,128)}, u32[]{:S(2)}) copy-start(f32[30,1536]{1,0:T(8,128)} %get-tuple-element.76) | copy-start | bytes 552964
  418.9 166.1 %copy-start.3 = (bf16[8,64,768]{2,1,0:T(8,128)(2,1)S(1)}, bf16[8,64,768]{2,1,0:T(8,128)(2,1)}, u32[]{:S(2)}) copy-start(bf16[8,64,768]{2,1,0:T(8,128)(2,1)} %get-tuple-element.94) | copy-start | bytes 2359300
Sparse Core Ops, SparseCore 0:
  270.7 140.7 all-reduce.4
Sparse Core Ops, SparseCore 1:
  274.7 74.5 reduce-scatter.4
  352.4 61.6 reduce-scatter.6
  417.5 61.6 reduce-scatter.10
  482.5 61.5 reduce-scatter.8
  546.8 31.8 all-reduce.6
